TPU v7x, 512 devices: a whole 4x8x8 slice. The times are simulated.
512 devices in a mesh: grp: 8 (over z), orb: 8 (over y_lo, core), slab: 8 (over x, y_hi).
Axes of the slice: x: 4, y: 8 (y_hi: 2, y_lo: 4; y = y_hi * 4 + y_lo), z: 8, core: 2. Of those that a mesh axis runs over, the one named last changes fastest.
Arguments:
- orbitals: float32 [512, 64, 64, 64], P(('grp', 'orb'), 'slab'), may hold values from -6 to 6
- offsets: int32 [512, 2], replicated, may hold values from 0 to 15
- pairs: int32 [512, 2], P(('grp', 'orb')), may hold values from 0 to 511, as said below
- live: int32 [512], P(('grp', 'orb')), may hold values from 0 to 1, as said below
Outputs:
- exchange: float32 [512, 64, 64, 64], P(('grp', 'orb'), 'slab')
Inputs may be any that keep to these rules, and one draw needn't show every extreme that they name: The 8 rows of one device of grp and orb (aligned blocks, in order) name as first orbital one of that device's 8 orbitals; the second orbital lies within 8 positions of the first on the cycle of 512 orbitals. In every block, row 0 pairs the device's lowest orbital with the orbital just below it on the cycle, and row 1 pairs the device's highest orbital with the orbital just above it. In each aligned block of 8 slots the live ones come first, at least two are live, and some block is all live.
All inputs are finite; a program needn't handle non-finite values.
Results may differ from a plain program's by a relative error of at most 0.0003.
Values sent between devices are 32-bit elements; how exact they have to be, the bound alone decides.
No kernel may reach another device: no remote copies, remote signals or barrier semaphores. Data moves between devices by JAX's collectives and lax.ppermute only.
A program may use at most 64 MiB of HBM per device.

v0:
```python
import jax
import jax.numpy as jnp
from jax import lax
from jax.sharding import PartitionSpec as P

PASSES = 8


DIAG = 6.25
THETA = 1.075
DELTA = 0.925


def padded_2(shard, sides, width):
    edges = {}
    for axis, dim in sides:
        size, length = (lax.axis_size(axis), shard.shape[dim])
        up = [(i, (i + 1) % size) for i in range(size)]
        last = lax.slice_in_dim(shard, length - width, length, axis=dim)
        leading = lax.slice_in_dim(shard, 0, width, axis=dim)
        edges[dim] = (
            lax.ppermute(last, axis, up),
            lax.ppermute(leading, axis, [(b, a) for a, b in up]),
        )
    done = []
    for _, dim in sides:
        low, high = edges[dim]
        around = [(width, width) if d in done else (0, 0) for d in range(shard.ndim)]
        shard = jnp.concatenate([jnp.pad(low, around), shard, jnp.pad(high, around)], axis=dim)
        done.append(dim)
    return shard


def items_in_groups(shard, axis, split_dim, concat_dim, work, item_dim, out_dim):

    def moved(group):
        return lax.all_to_all(group, axis, split_axis=split_dim, concat_axis=concat_dim, tiled=True)

    items = jax.tree.leaves(shard)[0].shape[item_dim]
    ends = [items * k // 2 for k in range(2 + 1)] if items % 2 == 0 else [0, items]
    groups = [
        jax.tree.map(lambda a: lax.slice_in_dim(a, low, high, axis=item_dim), shard)
        for low, high in zip(ends, ends[1:])
    ]
    arrived = [moved(group) for group in groups]
    made = [work(group) for group in arrived]
    return jax.tree.map(lambda *parts: jnp.concatenate(parts, axis=out_dim), *made)


def shifted(shard, axis, by):
    size = lax.axis_size(axis)
    return lax.ppermute(shard, axis, [(i, (i + by) % size) for i in range(size)])


def place_many(field, shift_y, shift_z):
    cells = field.shape[2]
    index = jnp.arange(cells, dtype=jnp.int32)
    move_y = (index[None, :, None] == index[None, None, :] - shift_y[:, None, None]).astype(
        jnp.float32
    )
    move_z = (index[None, :, None] == index[None, None, :] - shift_z[:, None, None]).astype(
        jnp.float32
    )
    moved = jnp.einsum("pxuz,puy->pxyz", field, move_y, precision=lax.Precision.HIGHEST)
    return jnp.einsum("pxyv,pvz->pxyz", moved, move_z, precision=lax.Precision.HIGHEST)


def apply_op(padded):
    core = padded[:, 1:-1]
    wider = jnp.pad(core, ((0, 0), (0, 0), (1, 1), (1, 1)))
    near = padded[:, 2:] + padded[:, :-2]
    near = near + wider[:, :, 2:, 1:-1] + wider[:, :, :-2, 1:-1]
    near = near + wider[:, :, 1:-1, 2:] + wider[:, :, 1:-1, :-2]
    return DIAG * core - near


def smooth(density, widen):
    sigma = THETA / DELTA
    resid = density
    value = jnp.zeros_like(density)
    step = resid / (DIAG * THETA)
    coef = 1.0 / sigma
    for turn in range(PASSES):
        value = value + step
        if turn < PASSES - 1:
            resid = resid - apply_op(widen(step))
            coef_new = 1.0 / (2.0 * sigma - coef)
            step = coef_new * coef * step + 2.0 * coef_new / DELTA * (resid / DIAG)
            coef = coef_new
    return value


def pad_first(field):
    return jnp.pad(field, ((0, 0), (1, 1), (0, 0), (0, 0)))


def solve_boxes(pieces):
    potential = smooth(pieces[0], pad_first)
    return lax.all_to_all(potential[None], "slab", split_axis=2, concat_axis=0, tiled=True)


def body(orbitals, offsets, pairs, live):
    orb_dev = orbitals.shape[0]
    slots = pairs.shape[0]
    total_orbs = offsets.shape[0]
    field_shape = orbitals.shape[1:]
    extended = padded_2(orbitals, ((("grp", "orb"), 0),), orb_dev)
    start = lax.axis_index(("grp", "orb")) * orb_dev - orb_dev
    first_local = jnp.mod(pairs[:, 0] - start, total_orbs)
    second_local = jnp.mod(pairs[:, 1] - start, total_orbs)
    table_ids = jnp.arange(total_orbs, dtype=jnp.int32)
    pick_first = (pairs[:, 0:1] == table_ids[None, :]).astype(jnp.int32)
    pick_second = (pairs[:, 1:2] == table_ids[None, :]).astype(jnp.int32)
    shift = jnp.sum((pick_second - pick_first)[:, :, None] * offsets[None, :, :], axis=1)
    rows = jnp.arange(3 * orb_dev, dtype=jnp.int32)
    select_first = (rows[:, None] == first_local[None, :]).astype(jnp.float32)
    select_second = (rows[:, None] == second_local[None, :]).astype(jnp.float32)
    flat_ext = extended.reshape(3 * orb_dev, -1)
    own = jnp.dot(select_first.T, flat_ext, precision=lax.Precision.HIGHEST).reshape(
        (slots,) + field_shape
    )
    other = jnp.dot(select_second.T, flat_ext, precision=lax.Precision.HIGHEST).reshape(
        (slots,) + field_shape
    )
    partner = place_many(other, shift[:, 0], shift[:, 1])
    density = own * partner
    width = lax.axis_size("slab")
    grouped = density.reshape((width, slots // width) + density.shape[1:])
    solved = items_in_groups(grouped, "slab", 0, 2, solve_boxes, 1, 1)
    potential = solved.reshape(density.shape)
    weight = live.astype(jnp.float32)[:, None, None, None]
    to_first = weight * potential * partner
    to_second = weight * place_many(potential * own, -shift[:, 0], -shift[:, 1])
    summed = jnp.dot(select_first, to_first.reshape(slots, -1), precision=lax.Precision.HIGHEST)
    summed = summed + jnp.dot(
        select_second, to_second.reshape(slots, -1), precision=lax.Precision.HIGHEST
    )
    summed = summed.reshape((3 * orb_dev,) + field_shape)
    before = summed[:orb_dev]
    middle = summed[orb_dev : 2 * orb_dev]
    after = summed[2 * orb_dev :]
    from_next = shifted(before, ("grp", "orb"), -1)
    from_prior = shifted(after, ("grp", "orb"), 1)
    return middle + from_next + from_prior


def solution(mesh):
    placed = (
        P(("grp", "orb"), "slab", None, None),
        P(),
        P(("grp", "orb"), None),
        P(("grp", "orb")),
    )
    return jax.shard_map(
        body,
        mesh=mesh,
        in_specs=placed,
        out_specs=P(("grp", "orb"), "slab", None, None),
        check_vma=False,
    )
```

profile of v0, /device:TPU:2, one launch (start us, length us, event | category | flops | bytes accessed | tf_op | source)
XLA Modules:
  0.0 278.0 jit_solution(16396989128261446074)
XLA Ops:
  0.0 1.9 collective-permute-start
  1.9 13.4 %collective-permute-start.1 = (f32[8,8,64,64]{3,2,1,0:T(8,128)}, f32[8,8,64,64]{3,2,1,0:T(8,128)}, u32[]{:S(2)}, u32[]{:S(2)}) collective-permute-start(f32[8,8,64,64]{3,2,1,0:T(8,128)} %param.4), channel_id=1, source_target_pairs={{8,0},{16,8},{24,16},{32,24},{40,32},{48,40},{56,48},{64,56},{72,6... | collective-permute-start | bytes 3145736 | tf_op jit(solution)/shard_map/ppermute | solution.py:23
  15.4 0.8 slice_bitcast_fusion.2
  16.1 0.1 convert_subtract_fusion
  16.2 0.8 multiply_reduce_fusion
  17.0 0.8 and_select_fusion.1
  17.8 0.1 iota_subtract_fusion.2
  17.9 37.4 %collective-permute-done = f32[8,8,64,64]{3,2,1,0:T(8,128)S(1)} collective-permute-done((f32[8,8,64,64]{3,2,1,0:T(8,128)}, f32[8,8,64,64]{3,2,1,0:T(8,128)S(1)}, u32[]{:S(2)}, u32[]{:S(2)}) %collective-permute-start) | collective-permute-done | bytes 1048608 | tf_op jit(solution)/shard_map/ppermute | solution.py:22
  55.2 0.0 collective-permute-done.1
  55.2 6.1 %pad_maximum_fusion = f32[24,8,64,64]{3,2,1,0:T(8,128)} fusion(f32[8,8,64,64]{3,2,1,0:T(8,128)} %collective-permute-done.1, f32[8,8,64,64]{3,2,1,0:T(8,128)} %param.4, f32[8,8,64,64]{3,2,1,0:T(8,128)S(1)} %collective-permute-done), kind=kLoop, calls=%fused_computation.1 | loop fusion | flops 1572864 | bytes 6291456 | tf_op jit(solution)/shard_map/concatenate | solution.py:29
  61.3 4.5 %reshape.246 = f32[24,32768]{1,0:T(8,128)S(1)} reshape(f32[24,8,64,64]{3,2,1,0:T(8,128)} %pad_maximum_fusion) | data formatting | bytes 6291456 | tf_op jit(solution)/shard_map/reshape | solution.py:118
  65.8 4.4 %dot_general.29 = f32[8,64,64,24]{2,1,0,3:T(8,128)} reshape(f32[32768,24]{0,1:T(8,128)S(1)} %bitcast.83) | data formatting | bytes 6291456 | tf_op jit(solution)/shard_map/dot_general | solution.py:119
  70.2 8.6 %fusion = f32[8,8,64,64]{3,0,2,1:T(8,128)S(1)} fusion(f32[8,64,64,24]{2,1,0,3:T(8,128)} %dot_general.29, s32[8]{0:T(128)S(1)} %get-tuple-element.21), kind=kOutput, calls=%fused_computation.2 | convolution fusion | flops 75497664 | bytes 4194336 | tf_op jit(solution)/shard_map/dot_general | solution.py:122
  78.9 5.7 %fusion.2 = f32[8,8,64,64]{3,0,2,1:T(8,128)S(1)} fusion(f32[8,64,64,24]{2,1,0,3:T(8,128)S(1)} %copy-done, s32[8]{0:T(128)S(1)} %get-tuple-element.20), kind=kOutput, calls=%fused_computation.4 | convolution fusion | flops 75497664 | bytes 4194336 | tf_op jit(solution)/shard_map/dot_general | solution.py:119
  84.6 0.0 copy-start.3
  84.6 1.5 fusion.57
  86.0 1.2 fusion.52
  87.2 0.0 copy-done.3
  87.2 0.0 copy-start.1
  87.2 1.4 fusion.56
  88.6 0.4 copy.27
  89.0 1.3 reshape.257
  90.4 33.9 %all_to_all.8 = f32[8,1,32768]{2,1,0:T(1,128)S(1)} all-to-all(f32[8,1,32768]{2,1,0:T(1,128)S(1)} %reshape.257), channel_id=1, replica_groups=mesh['grp'=8,'orb'=8,'slab'=8] {'slab'}, dimensions={0} | all-to-all | bytes 2097152 | tf_op jit(solution)/shard_map/all_to_all | solution.py:37
  124.3 0.6 broadcast.226
  124.9 3.2 %reduce = f32[8,32768]{1,0:T(8,128)S(1)} reduce(f32[8,1,32768]{2,1,0:T(1,128)S(1)} %all_to_all.8, f32[]{:T(128)} %broadcast.226), dimensions={1}, to_apply=%all_to_all.4.reduce_sub_computation | reduce | bytes 2097156 | tf_op jit(solution)/shard_map/all_to_all | solution.py:37
  128.1 0.8 reshape.258
  128.9 0.2 broadcast_multiply_fusion
  129.2 1.9 multiply_add_fusion.5
  131.1 2.1 multiply_add_fusion.4
  133.2 2.0 multiply_add_fusion.3
  135.2 2.2 multiply_add_fusion.2
  137.4 1.9 multiply_add_fusion.1
  139.3 1.4 copy-done.5
  140.7 0.6 copy-done.6
  141.3 3.1 %multiply_add_fusion = f32[1,64,64,64]{3,2,1,0:T(8,128)} fusion(f32[1,64,64,64]{3,2,1,0:T(8,128)S(1)} %get-tuple-element.6, f32[1,64,64,64]{3,2,1,0:T(8,128)S(1)} %get-tuple-element.7, f32[1,64,64,64]{3,2,1,0:T(8,128)S(1)} %get-tuple-element.5), kind=kLoop, calls=%fused_computation.93 | loop fusion | flops 3670016 | bytes 4194304 | tf_op jit(solution)/shard_map/add | solution.py:88
  144.5 18.4 %fusion.93 = f32[64,1,1,64,64]{4,3,2,1,0:T(8,128)} fusion(f32[1,64,64,64]{3,2,1,0:T(8,128)} %multiply_add_fusion, f32[1,64,64,64]{3,2,1,0:T(8,128)} %copy-done.6, f32[1,64,64,64]{3,2,1,0:T(8,128)} %copy-done.5, f32[1,64,64,64]{3,2,1,0:T(8,128)S(1)} %get-tuple-element.7, f32[1,64,64,64]{3,2,1,0:T(8,128)S(1)} %get-tuple-element.10, ...), kind=kLoop, calls=%fused_computation.145 | loop fusion | flops 8650752 | bytes 9437184
  162.9 0.0 copy-start.9
  162.9 3.4 %reshape.259 = f32[8,1,32768]{2,1,0:T(1,128)} reshape(f32[64,1,1,64,64]{4,3,2,1,0:T(8,128)} %fusion.93) | data formatting | bytes 2097152
  166.3 3.9 %all-to-all-start.1 = ((f32[8,1,32768]{2,1,0:T(1,128)}), f32[8,1,32768]{2,1,0:T(1,128)S(1)}, u32[]{:S(2)}, u32[]{:S(2)}) async-start(f32[8,1,32768]{2,1,0:T(1,128)} %reshape.259), calls=%async_computation.1 | async-start | bytes 2097152 | tf_op jit(solution)/shard_map/all_to_all | solution.py:99
  170.2 0.0 copy-done.9
  170.2 0.1 iota_subtract_fusion
  170.3 14.6 %all-to-all-done.1 = f32[8,1,32768]{2,1,0:T(1,128)S(1)} async-done(((f32[8,1,32768]{2,1,0:T(1,128)}), f32[8,1,32768]{2,1,0:T(1,128)S(1)}, u32[]{:S(2)}, u32[]{:S(2)}) %all-to-all-start.1) | async-done | bytes 1048608 | tf_op jit(solution)/shard_map/all_to_all | solution.py:99
  184.8 3.2 %reduce.1 = f32[8,32768]{1,0:T(8,128)S(1)} reduce(f32[8,1,32768]{2,1,0:T(1,128)S(1)} %all-to-all-done.1, f32[]{:T(128)} %broadcast.226), dimensions={1}, to_apply=%all_to_all.5.reduce_sub_computation | reduce | bytes 2097156 | tf_op jit(solution)/shard_map/all_to_all | solution.py:99
  188.0 0.8 reshape.260
  188.9 0.0 copy-start.2
  188.9 3.1 %copy_multiply_fusion = f32[8,8,64,64]{3,0,2,1:T(8,128)S(1)} fusion(f32[8,8,64,64]{3,0,2,1:T(8,128)} %copy-done.3, f32[8,8,64,64]{3,2,1,0:T(8,128)S(1)} %bitcast.81), kind=kLoop, calls=%fused_computation.86 | loop fusion | flops 262144 | bytes 3145728 | tf_op jit(solution)/shard_map/mul | solution.py:133
  192.0 0.0 copy-done.2
  192.0 1.8 multiply_multiply_fusion
  193.8 1.5 fusion.54
  195.2 2.5 fusion.59
  197.8 3.3 %reshape.250 = f32[8,32768]{1,0:T(8,128)} reshape(f32[8,8,64,64]{3,2,1,0:T(8,128)} %fusion.59) | data formatting | bytes 2097152 | tf_op jit(solution)/shard_map/reshape | solution.py:136
  201.1 0.7 reshape.249
  201.8 1.5 fusion.75
  203.3 0.0 copy-done.8
  203.3 1.6 convolution_add_fusion
  204.9 0.4 fusion.92
  205.3 2.2 slice.219
  207.5 1.9 collective-permute-start.2
  209.4 2.2 slice.221
  211.6 2.4 collective-permute-start.3
  214.0 0.8 slice.217
  214.8 26.1 %collective-permute-done.2 = f32[8,8,64,64]{3,2,1,0:T(8,128)} collective-permute-done((f32[8,8,64,64]{3,2,1,0:T(8,128)}, f32[8,8,64,64]{3,2,1,0:T(8,128)}, u32[]{:S(2)}, u32[]{:S(2)}) %collective-permute-start.2) | collective-permute-done | bytes 1048608 | tf_op jit(solution)/shard_map/ppermute | solution.py:52
  240.9 32.7 %collective-permute-done.3 = f32[8,8,64,64]{3,2,1,0:T(8,128)} collective-permute-done((f32[8,8,64,64]{3,2,1,0:T(8,128)}, f32[8,8,64,64]{3,2,1,0:T(8,128)}, u32[]{:S(2)}, u32[]{:S(2)}) %collective-permute-start.3) | collective-permute-done | bytes 1048608 | tf_op jit(solution)/shard_map/ppermute | solution.py:52
  273.6 4.2 %add_add_fusion = f32[8,8,64,64]{3,2,1,0:T(8,128)} fusion(f32[8,8,64,64]{3,2,1,0:T(8,128)} %collective-permute-done.3, f32[8,8,64,64]{3,2,1,0:T(8,128)S(1)} %slice.217, f32[8,8,64,64]{3,2,1,0:T(8,128)} %collective-permute-done.2), kind=kLoop, calls=%fused_computation.91 | loop fusion | flops 524288 | bytes 4194304 | tf_op jit(solution)/shard_map/add | solution.py:144
  (13 shorter events, 0.0 us)
Async XLA Ops:
  0.0 55.2 %collective-permute-start = (f32[8,8,64,64]{3,2,1,0:T(8,128)}, f32[8,8,64,64]{3,2,1,0:T(8,128)S(1)}, u32[]{:S(2)}, u32[]{:S(2)}) collective-permute-start(f32[8,8,64,64]{3,2,1,0:T(8,128)} %param.4), channel_id=1, source_target_pairs={{0,8},{8,16},{16,24},{24,32},{32,40},{40,48},{48,56},{56,64},{64,7... | collective-permute-start | bytes 3145736 | tf_op jit(solution)/shard_map/ppermute | solution.py:22
  1.9 53.3 %collective-permute-start.1 = (f32[8,8,64,64]{3,2,1,0:T(8,128)}, f32[8,8,64,64]{3,2,1,0:T(8,128)}, u32[]{:S(2)}, u32[]{:S(2)}) collective-permute-start(f32[8,8,64,64]{3,2,1,0:T(8,128)} %param.4), channel_id=1, source_target_pairs={{8,0},{16,8},{24,16},{32,24},{40,32},{48,40},{56,48},{64,56},{72,6... | collective-permute-start | bytes 3145736 | tf_op jit(solution)/shard_map/ppermute | solution.py:23
  70.2 8.7 %copy-start = (f32[8,64,64,24]{2,1,0,3:T(8,128)S(1)}, f32[8,64,64,24]{2,1,0,3:T(8,128)}, u32[]{:S(2)}) copy-start(f32[8,64,64,24]{2,1,0,3:T(8,128)} %dot_general.29) | copy-start | bytes 9437188
  84.6 2.7 copy-start.3
  87.2 1.4 copy-start.1
  131.1 2.1 copy-start.4
  139.3 1.4 copy-start.5
  139.3 2.0 copy-start.6
  162.9 7.3 %copy-start.9 = (s32[8]{0:T(128)S(1)}, s32[8]{0:T(128)}, u32[]{:S(2)}) copy-start(s32[8]{0:T(128)} %param.7) | copy-start | bytes 100
  166.3 18.6 %all-to-all-start.1 = ((f32[8,1,32768]{2,1,0:T(1,128)}), f32[8,1,32768]{2,1,0:T(1,128)S(1)}, u32[]{:S(2)}, u32[]{:S(2)}) async-start(f32[8,1,32768]{2,1,0:T(1,128)} %reshape.259), calls=%async_computation.1 | async-start | bytes 2097152 | tf_op jit(solution)/shard_map/all_to_all | solution.py:99
  188.9 3.1 %copy-start.2 = (f32[8,8,64,64]{3,2,1,0:T(8,128)S(1)}, f32[8,8,64,64]{3,2,1,0:T(8,128)}, u32[]{:S(2)}) copy-start(f32[8,8,64,64]{3,2,1,0:T(8,128)} %copy-done.1) | copy-start | bytes 3145732
  197.8 3.3 %copy-start.7 = (f32[8,8,64,64]{3,2,1,0:T(8,128)S(1)}, f32[8,8,64,64]{3,2,1,0:T(8,128)}, u32[]{:S(2)}) copy-start(f32[8,8,64,64]{3,2,1,0:T(8,128)} %multiply_multiply_fusion) | copy-start | bytes 3145732
  201.8 1.5 copy-start.8
  207.5 33.4 %collective-permute-start.2 = (f32[8,8,64,64]{3,2,1,0:T(8,128)}, f32[8,8,64,64]{3,2,1,0:T(8,128)}, u32[]{:S(2)}, u32[]{:S(2)}) collective-permute-start(f32[8,8,64,64]{3,2,1,0:T(8,128)} %slice.219), channel_id=1, source_target_pairs={{0,504},{8,0},{16,8},{24,16},{32,24},{40,32},{48,40},{56,48},{64,5... | collective-permute-start | bytes 3145736 | tf_op jit(solution)/shard_map/ppermute | solution.py:52
  211.6 62.0 %collective-permute-start.3 = (f32[8,8,64,64]{3,2,1,0:T(8,128)}, f32[8,8,64,64]{3,2,1,0:T(8,128)}, u32[]{:S(2)}, u32[]{:S(2)}) collective-permute-start(f32[8,8,64,64]{3,2,1,0:T(8,128)} %slice.221), channel_id=1, source_target_pairs={{0,8},{8,16},{16,24},{24,32},{32,40},{40,48},{48,56},{56,64},{64,7... | collective-permute-start | bytes 3145736 | tf_op jit(solution)/shard_map/ppermute | solution.py:52
where the time goes:
time: 283 us; the launch traced here: 278 us
  waiting for transfers between devices  111 us (39%)
  other arithmetic  56.6 us (20%)
  blocking collectives  33.9 us (12%)
  local copies, waits for them, and re-layouts  28.6 us (10%)
  matrix products  24.1 us (9%)
  starting transfers between devices  23.6 us (8%)
    ppermute x2, waiting for transfers between devices, shifted(): lax.ppermute(shard, axis, [(i, (i + by) % size) for i in range(size)])  58.8 us
    ppermute x1, waiting for transfers between devices, padded_2(): lax.ppermute(last, axis, up)  37.4 us
    all_to_all x1, blocking collectives, moved(): lax.all_to_all(group, axis, split_axis=split_dim, concat_axis=concat_dim,...  33.9 us
    unnamed x1, other arithmetic  18.4 us
    all_to_all x1, waiting for transfers between devices, solve_boxes(): lax.all_to_all(potential[None], 'slab', split_axis=2, concat_axis=0, tile...  14.6 us
    ppermute x1, starting transfers between devices, padded_2(): lax.ppermute(leading, axis, [(b, a) for a, b in up])  13.4 us
    add x6, other arithmetic, smooth(): step = coef_new * coef * step + 2.0 * coef_new / DELTA * (resid / DIAG)  13.2 us
    dot_general x1, matrix products, body(): jnp.dot(select_second.T, flat_ext, precision=lax.Precision.HIGHEST)  8.64 us
  transfers between devices with their start and end apart: 5, of which 4 were waited for; matrix products, arithmetic and copies ran while one was open for 2% of the time, Pallas kernels for 0%

commit v1 on v0

v1 whole, which is shorter than its diff:
```python
import functools

import jax
import jax.numpy as jnp
from jax import lax
from jax.experimental import pallas as pl
from jax.experimental.pallas import tpu as pltpu
from jax.sharding import PartitionSpec as P

PASSES = 8
DIAG = 6.25
THETA = 1.075
DELTA = 0.925

BOX = 64
LANES = 128
PAD = 16
ROWS = BOX + 2 * PAD
VMEM_BYTES = 40 * 1024 * 1024


def params():
    return pltpu.CompilerParams(vmem_limit_bytes=VMEM_BYTES)


def shifted(shard, axis, by):
    size = lax.axis_size(axis)
    return lax.ppermute(shard, axis, [(i, (i + by) % size) for i in range(size)])


def lane_index(shape):
    return lax.broadcasted_iota(jnp.int32, shape, len(shape) - 1)


def moved_z(field, by):
    z = lane_index(field.shape) & (BOX - 1)
    source = z - by
    rolled = pltpu.roll(field, jnp.where(by < 0, by + LANES, by), 1)
    return jnp.where((source >= 0) & (source < BOX), rolled, 0.0)


def pack_kernel(field_ref, out_ref):
    half = field_ref.shape[1] // 2
    out_ref[...] = jnp.concatenate([field_ref[:, :half], field_ref[:, half:]], axis=-1)


def pack(orbitals):
    orbs, planes = orbitals.shape[:2]
    return pl.pallas_call(
        pack_kernel,
        grid=(2,),
        in_specs=[pl.BlockSpec((orbs // 2, planes, BOX, BOX), lambda i: (i, 0, 0, 0))],
        out_specs=pl.BlockSpec((orbs // 2, planes // 2, BOX, LANES), lambda i: (i, 0, 0, 0)),
        out_shape=jax.ShapeDtypeStruct((orbs, planes // 2, BOX, LANES), jnp.float32),
        compiler_params=params(),
    )(orbitals)


def finish_kernel(mid_ref, next_ref, prior_ref, out_ref):
    half = mid_ref.shape[1]
    total = mid_ref[...] + next_ref[...] + prior_ref[...]
    out_ref[:, :half] = total[..., :BOX]
    out_ref[:, half:] = total[..., BOX:]


def finish(middle, from_next, from_prior):
    orbs, half = middle.shape[:2]
    spec = pl.BlockSpec((orbs // 2, half, BOX, LANES), lambda i: (i, 0, 0, 0))
    return pl.pallas_call(
        finish_kernel,
        grid=(2,),
        in_specs=[spec] * 3,
        out_specs=pl.BlockSpec((orbs // 2, 2 * half, BOX, BOX), lambda i: (i, 0, 0, 0)),
        out_shape=jax.ShapeDtypeStruct((orbs, 2 * half, BOX, BOX), jnp.float32),
        compiler_params=params(),
    )(middle, from_next, from_prior)


def clear_pads(ext):
    zeros = jnp.zeros((ext.shape[1], PAD, LANES), jnp.float32)

    @pl.loop(0, ext.shape[0])
    def _(orb):
        ext[orb, :, :PAD] = zeros
        ext[orb, :, PAD + BOX :] = zeros


def fetch(refs, ext, sems):
    copies = []
    for k, ref in enumerate(refs):
        orbs = ref.shape[0]
        copies.append(
            pltpu.make_async_copy(
                ref, ext.at[pl.ds(k * orbs, orbs), :, pl.ds(PAD, BOX), :], sems.at[k]
            )
        )
    for copy in copies:
        copy.start()
    return copies


def density_kernel(table_ref, prev_ref, own_ref, next_ref, out_ref, ext, sems):
    copies = fetch((prev_ref, own_ref, next_ref), ext, sems)
    clear_pads(ext)
    for copy in copies:
        copy.wait()
    slots, planes = out_ref.shape[:2]

    @pl.loop(0, slots)
    def _(slot):
        first = table_ref[0, slot]
        second = table_ref[1, slot]
        by_y = table_ref[2, slot]
        by_z = table_ref[3, slot]
        for x in range(planes):
            partner = moved_z(ext[second, x, pl.ds(PAD - by_y, BOX), :], by_z)
            out_ref[slot, x] = ext[first, x, PAD : PAD + BOX, :] * partner


def densities(table, prev, own, after):
    slots = table.shape[1]
    orbs, planes = own.shape[:2]
    return pl.pallas_call(
        density_kernel,
        in_specs=[pl.BlockSpec(memory_space=pltpu.SMEM)] + [pl.BlockSpec(memory_space=pl.ANY)] * 3,
        out_specs=pl.BlockSpec(memory_space=pltpu.VMEM),
        out_shape=jax.ShapeDtypeStruct((slots, planes, BOX, LANES), jnp.float32),
        scratch_shapes=[
            pltpu.VMEM((3 * orbs, planes, ROWS, LANES), jnp.float32),
            pltpu.SemaphoreType.DMA((3,)),
        ],
        compiler_params=params(),
    )(table, prev, own, after)


def exchange_kernel(
    table_ref, pot_ref, prev_ref, own_ref, next_ref, before_ref, mid_ref, after_ref, ext, acc, moved, sems
):
    copies = fetch((prev_ref, own_ref, next_ref), ext, sems)
    clear_pads(ext)
    orbs, planes = mid_ref.shape[:2]
    zeros = jnp.zeros((planes, BOX, LANES), jnp.float32)

    @pl.loop(0, 3 * orbs)
    def _(orb):
        acc[orb] = zeros

    for x in range(planes):
        moved[x, :PAD] = jnp.zeros((PAD, LANES), jnp.float32)
        moved[x, PAD + BOX :] = jnp.zeros((PAD, LANES), jnp.float32)
    for copy in copies:
        copy.wait()

    @pl.loop(0, table_ref.shape[1])
    def _(slot):
        first = table_ref[0, slot]
        second = table_ref[1, slot]
        by_y = table_ref[2, slot]
        by_z = table_ref[3, slot]
        weight = table_ref[4, slot].astype(jnp.float32)
        for x in range(planes):
            pot = weight * pot_ref[slot, x]
            partner = moved_z(ext[second, x, pl.ds(PAD - by_y, BOX), :], by_z)
            acc[first, x] += pot * partner
            moved[x, PAD : PAD + BOX] = moved_z(pot * ext[first, x, PAD : PAD + BOX, :], -by_z)
        for x in range(planes):
            acc[second, x] += moved[x, pl.ds(PAD + by_y, BOX), :]

    before_ref[...] = acc[:orbs]
    mid_ref[...] = acc[orbs : 2 * orbs]
    after_ref[...] = acc[2 * orbs :]


def exchange_terms(table, potential, prev, own, after):
    orbs, planes = own.shape[:2]
    vmem = pl.BlockSpec(memory_space=pltpu.VMEM)
    return pl.pallas_call(
        exchange_kernel,
        in_specs=[pl.BlockSpec(memory_space=pltpu.SMEM), vmem] + [pl.BlockSpec(memory_space=pl.ANY)] * 3,
        out_specs=[vmem] * 3,
        out_shape=[jax.ShapeDtypeStruct(own.shape, jnp.float32)] * 3,
        scratch_shapes=[
            pltpu.VMEM((3 * orbs, planes, ROWS, LANES), jnp.float32),
            pltpu.VMEM((3 * orbs, planes, BOX, LANES), jnp.float32),
            pltpu.VMEM((planes, ROWS, LANES), jnp.float32),
            pltpu.SemaphoreType.DMA((3,)),
        ],
        compiler_params=params(),
    )(table, potential, prev, own, after)


EDGE = 8
HALF = BOX // 2


def coefficients():
    sigma = THETA / DELTA
    coef = 1.0 / sigma
    made = []
    for _ in range(PASSES - 1):
        new = 1.0 / (2.0 * sigma - coef)
        made.append((new * coef, 2.0 * new / (DELTA * DIAG)))
        coef = new
    return made


def solve_kernel(dens_ref, out_ref, resid, value, step_a, step_b):
    slabs, planes = dens_ref.shape[:2]
    lane = lane_index((BOX, LANES))
    low = lane < BOX
    z = lane & (BOX - 1)
    not_first = z > 0
    not_last = z < BOX - 1
    core = slice(EDGE, EDGE + BOX)

    for step in (step_a, step_b):

        @pl.loop(0, HALF + 2)
        def _(x):
            step[x, :EDGE] = jnp.zeros((EDGE, LANES), jnp.float32)
            step[x, EDGE + BOX :] = jnp.zeros((EDGE, LANES), jnp.float32)

    def seam(step):
        last = pltpu.roll(step[HALF, core, :], BOX, 1)
        step[0, core, :] = jnp.where(low, 0.0, last)
        leading = pltpu.roll(step[1, core, :], BOX, 1)
        step[HALF + 1, core, :] = jnp.where(low, leading, 0.0)

    @pl.loop(0, slabs // 2)
    def _(slab):
        for k in range(planes):
            one = dens_ref[slab, k]
            two = dens_ref[slab + slabs // 2, k]
            near = jnp.where(low, one, pltpu.roll(two, BOX, 1))
            far = jnp.where(low, pltpu.roll(one, BOX, 1), two)
            for x, plane in ((2 * planes * slab + k, near), (2 * planes * slab + planes + k, far)):
                start = plane * (1.0 / (DIAG * THETA))
                resid[x] = plane
                value[x] = start
                step_a[x + 1, core, :] = start

    seam(step_a)
    old, new = step_a, step_b
    for keep, add in coefficients():

        @pl.loop(0, HALF, unroll=2)
        def _(x):
            mid = old[x + 1, core, :]
            near = old[x, core, :] + old[x + 2, core, :]
            near = near + old[x + 1, EDGE - 1 : EDGE - 1 + BOX, :]
            near = near + old[x + 1, EDGE + 1 : EDGE + 1 + BOX, :]
            near = near + jnp.where(not_first, pltpu.roll(mid, 1, 1), 0.0)
            near = near + jnp.where(not_last, pltpu.roll(mid, LANES - 1, 1), 0.0)
            left = (resid[x] - DIAG * mid) + near
            resid[x] = left
            fresh = keep * mid + add * left
            new[x + 1, core, :] = fresh
            value[x] += fresh

        seam(new)
        old, new = new, old

    @pl.loop(0, slabs // 2)
    def _(slab):
        for k in range(planes):
            near = value[2 * planes * slab + k]
            far = value[2 * planes * slab + planes + k]
            out_ref[slab, k] = jnp.where(low, near, pltpu.roll(far, BOX, 1))
            out_ref[slab + slabs // 2, k] = jnp.where(low, pltpu.roll(near, BOX, 1), far)


def solve(density):
    vmem = pl.BlockSpec(memory_space=pltpu.VMEM)
    return pl.pallas_call(
        solve_kernel,
        in_specs=[vmem],
        out_specs=vmem,
        out_shape=jax.ShapeDtypeStruct(density.shape, jnp.float32),
        scratch_shapes=[
            pltpu.VMEM((HALF, BOX, LANES), jnp.float32),
            pltpu.VMEM((HALF, BOX, LANES), jnp.float32),
            pltpu.VMEM((HALF + 2, BOX + 2 * EDGE, LANES), jnp.float32),
            pltpu.VMEM((HALF + 2, BOX + 2 * EDGE, LANES), jnp.float32),
        ],
        compiler_params=params(),
    )(density)


def slot_table(offsets, pairs, live, orb_dev):
    total_orbs = offsets.shape[0]
    start = lax.axis_index(("grp", "orb")) * orb_dev - orb_dev
    local = jnp.mod(pairs - start, total_orbs)
    ids = jnp.arange(total_orbs, dtype=jnp.int32)
    pick_first = (pairs[:, 0:1] == ids[None, :]).astype(jnp.int32)
    pick_second = (pairs[:, 1:2] == ids[None, :]).astype(jnp.int32)
    shift = jnp.sum((pick_second - pick_first)[:, :, None] * offsets[None, :, :], axis=1)
    return jnp.concatenate([local.T, shift.T, live[None, :]], axis=0)


def swap(slabs):
    return lax.all_to_all(slabs, "slab", split_axis=0, concat_axis=0, tiled=True)


def body(orbitals, offsets, pairs, live):
    ring = ("grp", "orb")
    table = slot_table(offsets, pairs, live, orbitals.shape[0])
    own = pack(orbitals)
    prev = shifted(own, ring, 1)
    after = shifted(own, ring, -1)
    potential = swap(solve(swap(densities(table, prev, own, after))))
    to_prior, middle, to_next = exchange_terms(table, potential, prev, own, after)
    return finish(middle, shifted(to_prior, ring, -1), shifted(to_next, ring, 1))


def solution(mesh):
    placed = (
        P(("grp", "orb"), "slab", None, None),
        P(),
        P(("grp", "orb"), None),
        P(("grp", "orb")),
    )
    return jax.shard_map(
        body,
        mesh=mesh,
        in_specs=placed,
        out_specs=P(("grp", "orb"), "slab", None, None),
        check_vma=False,
    )
```

time: 283 us -> 150 us (0.53); the launches traced: 278 us -> 150 us
  other arithmetic: 56.6 us -> 0.24 us
  waiting for transfers between devices: 111 us -> 60 us
  local copies, waits for them, and re-layouts: 28.6 us -> 1.61 us
  matrix products: 24.1 us -> 0 us
  Pallas kernels: 0 us -> 20.5 us
  blocking collectives: 33.9 us -> 47.9 us
  starting transfers between devices: 23.6 us -> 19.7 us
    ppermute x2 -> x0, waiting for transfers between devices: 37.4 us -> none  [the longest x1 37.4 us: padded_2(): lax.ppermute(last, axis, up)]
    dot_general x8 -> x0, matrix products: 24.1 us -> none  [the longest x1 8.64 us: body(): jnp.dot(select_second.T, flat_ext, precision=lax.Precision.HIGHEST)]
    pallas_call x0 -> x5, Pallas kernels: none -> 20.5 us  [the longest x1 14 us: solve(): pl.pallas_call(solve_kernel, in_specs=[vmem], out_specs=vmem, out_shape=j...]
    unnamed x1 -> x0, other arithmetic: 18.4 us -> none
    add x7 -> x0, other arithmetic: 17.4 us -> none  [the longest x6 13.2 us: smooth(): step = coef_new * coef * step + 2.0 * coef_new / DELTA * (resid / DIAG)]
    ppermute x2 -> x4, starting transfers between devices: 4.31 us -> 19.7 us  [shifted(): lax.ppermute(shard, axis, [(i, (i + by) % size) for i in range(size)])]
    ppermute x2 -> x0, starting transfers between devices: 15.3 us -> none  [the longest x1 13.4 us: padded_2(): lax.ppermute(leading, axis, [(b, a) for a, b in up])]
    all_to_all x1 -> x0, waiting for transfers between devices: 14.6 us -> none  [solve_boxes(): lax.all_to_all(potential[None], 'slab', split_axis=2, concat_axis=0, tile...]
  transfers between devices with their start and end apart: 5 -> 4, of which waited for: 4 -> 4; matrix products, arithmetic and copies ran while one was open for 2% -> 0% of each run, Pallas kernels for 0% -> 0%
where the time goes in v1:
time: 150 us
  waiting for transfers between devices  60 us (40%)
  blocking collectives  47.9 us (32%)
  Pallas kernels  20.5 us (14%)
  starting transfers between devices  19.7 us (13%)
  local copies, waits for them, and re-layouts  1.61 us (1%)
    ppermute x4, waiting for transfers between devices, shifted(): lax.ppermute(shard, axis, [(i, (i + by) % size) for i in range(size)])  60 us
    all_to_all x2, blocking collectives, swap(): lax.all_to_all(slabs, 'slab', split_axis=0, concat_axis=0, tiled=True)  47.9 us
    ppermute x4, starting transfers between devices, shifted(): lax.ppermute(shard, axis, [(i, (i + by) % size) for i in range(size)])  19.7 us
    pallas_call x1, Pallas kernels, solve(): pl.pallas_call(solve_kernel, in_specs=[vmem], out_specs=vmem, out_shape=j...  14 us
  transfers between devices with their start and end apart: 4, of which 4 were waited for; matrix products, arithmetic and copies ran while one was open for 0% of the time, Pallas kernels for 0%

profile of v1, /device:TPU:2, one launch (start us, length us, event | category | flops | bytes accessed | tf_op | source)
XLA Modules:
  0.0 150.1 jit_solution(11287545151978427427)
XLA Ops:
  0.0 0.0 copy-start
  0.0 1.6 %copy-done = f32[8,8,64,64]{3,2,1,0:T(8,128)S(1)} copy-done((f32[8,8,64,64]{3,2,1,0:T(8,128)S(1)}, f32[8,8,64,64]{3,2,1,0:T(8,128)}, u32[]{:S(2)}) %copy-start) | copy-done | bytes 1048600
  1.6 0.0 copy-start.1
  1.6 0.0 copy-start.2
  1.6 0.0 copy-start.3
  1.6 0.4 shard_map.46.own_ref
  2.0 13.4 %collective-permute-start.1 = (f32[8,4,64,128]{3,2,1,0:T(8,128)S(1)}, f32[8,4,64,128]{3,2,1,0:T(8,128)S(1)}, u32[]{:S(2)}, u32[]{:S(2)}) collective-permute-start(f32[8,4,64,128]{3,2,1,0:T(8,128)S(1)} %shard_map.46.own_ref), channel_id=1, source_target_pairs={{0,504},{8,0},{16,8},{24,16},{32,24},{40,32},{48,40},{56,48},{64,5... | collective-permute-start | bytes 3145736 | tf_op jit(solution)/shard_map/ppermute | solution.py:28
  15.5 1.9 %collective-permute-start = (f32[8,4,64,128]{3,2,1,0:T(8,128)S(1)}, f32[8,4,64,128]{3,2,1,0:T(8,128)S(1)}, u32[]{:S(2)}, u32[]{:S(2)}) collective-permute-start(f32[8,4,64,128]{3,2,1,0:T(8,128)S(1)} %shard_map.46.own_ref), channel_id=1, source_target_pairs={{0,8},{8,16},{16,24},{24,32},{32,40},{40,48},{48,56},{56,64},{64,7... | collective-permute-start | bytes 3145736 | tf_op jit(solution)/shard_map/ppermute | solution.py:28
  17.4 0.0 copy-done.1
  17.4 0.1 convert_subtract_fusion
  17.5 0.0 copy-done.2
  17.5 0.1 multiply_reduce_fusion
  17.7 0.0 copy-done.3
  17.7 12.8 %collective-permute-done.1.next_ref = f32[8,4,64,128]{3,2,1,0:T(8,128)S(1)} collective-permute-done((f32[8,4,64,128]{3,2,1,0:T(8,128)S(1)}, f32[8,4,64,128]{3,2,1,0:T(8,128)S(1)}, u32[]{:S(2)}, u32[]{:S(2)}) %collective-permute-start.1) | collective-permute-done | bytes 1048608 | tf_op jit(solution)/shard_map/ppermute | solution.py:28
  30.4 9.6 %collective-permute-done.prev_ref = f32[8,4,64,128]{3,2,1,0:T(8,128)S(1)} collective-permute-done((f32[8,4,64,128]{3,2,1,0:T(8,128)S(1)}, f32[8,4,64,128]{3,2,1,0:T(8,128)S(1)}, u32[]{:S(2)}, u32[]{:S(2)}) %collective-permute-start) | collective-permute-done | bytes 1048608 | tf_op jit(solution)/shard_map/ppermute | solution.py:28
  40.0 1.8 %shard_map.47 = f32[8,4,64,128]{3,2,1,0:T(8,128)S(1)} custom-call(s32[5,8]{1,0:T(8,128)S(1)} %pad_add_fusion.table_ref, f32[8,4,64,128]{3,2,1,0:T(8,128)S(1)} %collective-permute-done.prev_ref, f32[8,4,64,128]{3,2,1,0:T(8,128)S(1)} %shard_map.46.own_ref, f32[8,4,64,128]{3,2,1,0:T(8,128)S(1)} %collective-permute-done.1.next_ref), custom_call_target="tpu_custom_call" | custom-call | tf_op jit(solution)/shard_map/pallas_call | solution.py:123
  41.9 21.7 %all_to_all.10.dens_ref = f32[8,4,64,128]{3,2,1,0:T(8,128)S(1)} all-to-all(f32[8,4,64,128]{3,2,1,0:T(8,128)S(1)} %shard_map.47), channel_id=1, replica_groups=mesh['grp'=8,'orb'=8,'slab'=8] {'slab'}, dimensions={0} | all-to-all | bytes 2097152 | tf_op jit(solution)/shard_map/all_to_all | solution.py:301
  63.6 14.0 %shard_map.48 = f32[8,4,64,128]{3,2,1,0:T(8,128)S(1)} custom-call(f32[8,4,64,128]{3,2,1,0:T(8,128)S(1)} %all_to_all.10.dens_ref), custom_call_target="tpu_custom_call" | custom-call | tf_op jit(solution)/shard_map/pallas_call | solution.py:274
  77.6 26.2 %all_to_all.11.pot_ref = f32[8,4,64,128]{3,2,1,0:T(8,128)S(1)} all-to-all(f32[8,4,64,128]{3,2,1,0:T(8,128)S(1)} %shard_map.48), channel_id=1, replica_groups=mesh['grp'=8,'orb'=8,'slab'=8] {'slab'}, dimensions={0} | all-to-all | bytes 2097152 | tf_op jit(solution)/shard_map/all_to_all | solution.py:301
  103.8 2.6 %shard_map.49 = (f32[8,4,64,128]{3,2,1,0:T(8,128)S(1)}, f32[8,4,64,128]{3,2,1,0:T(8,128)S(1)}, f32[8,4,64,128]{3,2,1,0:T(8,128)S(1)}) custom-call(s32[5,8]{1,0:T(8,128)S(1)} %pad_add_fusion.table_ref, f32[8,4,64,128]{3,2,1,0:T(8,128)S(1)} %all_to_all.11.pot_ref, f32[8,4,64,128]{3,2,1,0:T(8,128)S(1)} %collective-permute-done.prev_ref, ...), custom_call_target="tpu_custom_call" | custom-call | tf_op jit(solution)/shard_map/pallas_call | solution.py:177
  106.5 1.9 %collective-permute-start.2 = (f32[8,4,64,128]{3,2,1,0:T(8,128)S(1)}, f32[8,4,64,128]{3,2,1,0:T(8,128)S(1)}, u32[]{:S(2)}, u32[]{:S(2)}) collective-permute-start(f32[8,4,64,128]{3,2,1,0:T(8,128)S(1)} %get-tuple-element.9), channel_id=1, source_target_pairs={{0,504},{8,0},{16,8},{24,16},{32,24},{40,32},{48,40},{56,48},{64,5... | collective-permute-start | bytes 3145736 | tf_op jit(solution)/shard_map/ppermute | solution.py:28
  108.4 2.4 %collective-permute-start.3 = (f32[8,4,64,128]{3,2,1,0:T(8,128)S(1)}, f32[8,4,64,128]{3,2,1,0:T(8,128)S(1)}, u32[]{:S(2)}, u32[]{:S(2)}) collective-permute-start(f32[8,4,64,128]{3,2,1,0:T(8,128)S(1)} %get-tuple-element.10), channel_id=1, source_target_pairs={{0,8},{8,16},{16,24},{24,32},{32,40},{40,48},{48,56},{56,64},{64,7... | collective-permute-start | bytes 3145736 | tf_op jit(solution)/shard_map/ppermute | solution.py:28
  110.8 17.5 %collective-permute-done.2.next_ref = f32[8,4,64,128]{3,2,1,0:T(8,128)S(1)} collective-permute-done((f32[8,4,64,128]{3,2,1,0:T(8,128)S(1)}, f32[8,4,64,128]{3,2,1,0:T(8,128)S(1)}, u32[]{:S(2)}, u32[]{:S(2)}) %collective-permute-start.2) | collective-permute-done | bytes 1048608 | tf_op jit(solution)/shard_map/ppermute | solution.py:28
  128.4 20.1 %collective-permute-done.3.prior_ref = f32[8,4,64,128]{3,2,1,0:T(8,128)S(1)} collective-permute-done((f32[8,4,64,128]{3,2,1,0:T(8,128)S(1)}, f32[8,4,64,128]{3,2,1,0:T(8,128)S(1)}, u32[]{:S(2)}, u32[]{:S(2)}) %collective-permute-start.3) | collective-permute-done | bytes 1048608 | tf_op jit(solution)/shard_map/ppermute | solution.py:28
  148.5 1.6 %shard_map.50 = f32[8,8,64,64]{3,2,1,0:T(8,128)} custom-call(f32[8,4,64,128]{3,2,1,0:T(8,128)S(1)} %get-tuple-element.8.mid_ref, f32[8,4,64,128]{3,2,1,0:T(8,128)S(1)} %collective-permute-done.2.next_ref, f32[8,4,64,128]{3,2,1,0:T(8,128)S(1)} %collective-permute-done.3.prior_ref), custom_call_target="tpu_custom_call" | custom-call | tf_op jit(solution)/shard_map/pallas_call | solution.py:69
  (3 shorter events, 0.0 us)
Async XLA Ops:
  0.0 1.6 %copy-start = (f32[8,8,64,64]{3,2,1,0:T(8,128)S(1)}, f32[8,8,64,64]{3,2,1,0:T(8,128)}, u32[]{:S(2)}) copy-start(f32[8,8,64,64]{3,2,1,0:T(8,128)} %field_ref.1) | copy-start | bytes 3145732
  1.6 15.8 %copy-start.1 = (s32[8,2]{0,1:T(2,128)S(1)}, s32[8,2]{0,1:T(2,128)}, u32[]{:S(2)}) copy-start(s32[8,2]{0,1:T(2,128)} %param.6) | copy-start | bytes 196
  1.6 15.9 %copy-start.2 = (s32[512,2]{0,1:T(2,128)S(1)}, s32[512,2]{0,1:T(2,128)}, u32[]{:S(2)}) copy-start(s32[512,2]{0,1:T(2,128)} %param.5) | copy-start | bytes 12292
  1.6 16.1 %copy-start.3 = (s32[8]{0:T(128)S(1)}, s32[8]{0:T(128)}, u32[]{:S(2)}) copy-start(s32[8]{0:T(128)} %param.7) | copy-start | bytes 100
  2.0 28.4 %collective-permute-start.1 = (f32[8,4,64,128]{3,2,1,0:T(8,128)S(1)}, f32[8,4,64,128]{3,2,1,0:T(8,128)S(1)}, u32[]{:S(2)}, u32[]{:S(2)}) collective-permute-start(f32[8,4,64,128]{3,2,1,0:T(8,128)S(1)} %shard_map.46.own_ref), channel_id=1, source_target_pairs={{0,504},{8,0},{16,8},{24,16},{32,24},{40,32},{48,40},{56,48},{64,5... | collective-permute-start | bytes 3145736 | tf_op jit(solution)/shard_map/ppermute | solution.py:28
  15.5 24.6 %collective-permute-start = (f32[8,4,64,128]{3,2,1,0:T(8,128)S(1)}, f32[8,4,64,128]{3,2,1,0:T(8,128)S(1)}, u32[]{:S(2)}, u32[]{:S(2)}) collective-permute-start(f32[8,4,64,128]{3,2,1,0:T(8,128)S(1)} %shard_map.46.own_ref), channel_id=1, source_target_pairs={{0,8},{8,16},{16,24},{24,32},{32,40},{40,48},{48,56},{56,64},{64,7... | collective-permute-start | bytes 3145736 | tf_op jit(solution)/shard_map/ppermute | solution.py:28
  106.5 21.9 %collective-permute-start.2 = (f32[8,4,64,128]{3,2,1,0:T(8,128)S(1)}, f32[8,4,64,128]{3,2,1,0:T(8,128)S(1)}, u32[]{:S(2)}, u32[]{:S(2)}) collective-permute-start(f32[8,4,64,128]{3,2,1,0:T(8,128)S(1)} %get-tuple-element.9), channel_id=1, source_target_pairs={{0,504},{8,0},{16,8},{24,16},{32,24},{40,32},{48,40},{56,48},{64,5... | collective-permute-start | bytes 3145736 | tf_op jit(solution)/shard_map/ppermute | solution.py:28
  108.4 40.1 %collective-permute-start.3 = (f32[8,4,64,128]{3,2,1,0:T(8,128)S(1)}, f32[8,4,64,128]{3,2,1,0:T(8,128)S(1)}, u32[]{:S(2)}, u32[]{:S(2)}) collective-permute-start(f32[8,4,64,128]{3,2,1,0:T(8,128)S(1)} %get-tuple-element.10), channel_id=1, source_target_pairs={{0,8},{8,16},{16,24},{24,32},{32,40},{40,48},{48,56},{56,64},{64,7... | collective-permute-start | bytes 3145736 | tf_op jit(solution)/shard_map/ppermute | solution.py:28

commit v2 on v1

v2 whole, which is shorter than its diff:
```python
import functools

import jax
import jax.numpy as jnp
from jax import lax
from jax.experimental import pallas as pl
from jax.experimental.pallas import tpu as pltpu
from jax.sharding import PartitionSpec as P

PASSES = 8
DIAG = 6.25
THETA = 1.075
DELTA = 0.925

BOX = 64
LANES = 128
PAD = 16
ROWS = BOX + 2 * PAD
VMEM_BYTES = 40 * 1024 * 1024


def params():
    return pltpu.CompilerParams(vmem_limit_bytes=VMEM_BYTES)


def shifted(shard, axis, by):
    size = lax.axis_size(axis)
    return lax.ppermute(shard, axis, [(i, (i + by) % size) for i in range(size)])


def lane_index(shape):
    return lax.broadcasted_iota(jnp.int32, shape, len(shape) - 1)


def moved_z(field, by):
    z = lane_index(field.shape) & (BOX - 1)
    source = z - by
    rolled = pltpu.roll(field, jnp.where(by < 0, by + LANES, by), 1)
    return jnp.where((source >= 0) & (source < BOX), rolled, 0.0)


def pack_kernel(field_ref, out_ref):
    half = field_ref.shape[1] // 2
    out_ref[...] = jnp.concatenate([field_ref[:, :half], field_ref[:, half:]], axis=-1)


def pack(orbitals):
    orbs, planes = orbitals.shape[:2]
    return pl.pallas_call(
        pack_kernel,
        grid=(2,),
        in_specs=[pl.BlockSpec((orbs // 2, planes, BOX, BOX), lambda i: (i, 0, 0, 0))],
        out_specs=pl.BlockSpec((orbs // 2, planes // 2, BOX, LANES), lambda i: (i, 0, 0, 0)),
        out_shape=jax.ShapeDtypeStruct((orbs, planes // 2, BOX, LANES), jnp.float32),
        compiler_params=params(),
    )(orbitals)


def finish_kernel(mid_ref, next_ref, prior_ref, out_ref):
    half = mid_ref.shape[1]
    total = mid_ref[...] + next_ref[...] + prior_ref[...]
    out_ref[:, :half] = total[..., :BOX]
    out_ref[:, half:] = total[..., BOX:]


def finish(middle, from_next, from_prior):
    orbs, half = middle.shape[:2]
    spec = pl.BlockSpec((orbs // 2, half, BOX, LANES), lambda i: (i, 0, 0, 0))
    return pl.pallas_call(
        finish_kernel,
        grid=(2,),
        in_specs=[spec] * 3,
        out_specs=pl.BlockSpec((orbs // 2, 2 * half, BOX, BOX), lambda i: (i, 0, 0, 0)),
        out_shape=jax.ShapeDtypeStruct((orbs, 2 * half, BOX, BOX), jnp.float32),
        compiler_params=params(),
    )(middle, from_next, from_prior)


FIRST, SECOND, BY_Y, BY_Z, LIVE, SLAB = range(6)


def clear_pads(ext):
    zeros = jnp.zeros((ext.shape[1], PAD, LANES), jnp.float32)

    @pl.loop(0, ext.shape[0])
    def _(orb):
        ext[orb, :, :PAD] = zeros
        ext[orb, :, PAD + BOX :] = zeros


def fetch(refs, ext, sems):
    copies = []
    for k, ref in enumerate(refs):
        orbs = ref.shape[0]
        copies.append(
            pltpu.make_async_copy(
                ref, ext.at[pl.ds(k * orbs, orbs), :, pl.ds(PAD, BOX), :], sems.at[k]
            )
        )
    for copy in copies:
        copy.start()
    return copies


def swapped(field):
    return pltpu.roll(field, LANES // 2, 1)


def density_kernel(table_ref, prev_ref, own_ref, next_ref, *rest):
    out_refs, ext, sems = rest[:-2], rest[-2], rest[-1]
    copies = fetch((prev_ref, own_ref, next_ref), ext, sems)
    clear_pads(ext)
    for copy in copies:
        copy.wait()
    planes = own_ref.shape[1]
    low = lane_index((BOX, LANES)) < BOX

    def density(slot, x):
        first = table_ref[FIRST, slot]
        second = table_ref[SECOND, slot]
        partner = ext[second, x, pl.ds(PAD - table_ref[BY_Y, slot], BOX), :]
        return ext[first, x, PAD : PAD + BOX, :] * moved_z(partner, table_ref[BY_Z, slot])

    done = 0
    for out_ref in out_refs:
        count = out_ref.shape[0]

        @pl.loop(0, count)
        def _(pair):
            slot = 2 * (done + pair)
            for x in range(planes):
                one = density(slot, x)
                two = density(slot + 1, x)
                out_ref[pair, x] = jnp.where(low, one, swapped(two))
                out_ref[pair, planes + x] = jnp.where(low, swapped(one), two)

        done += count


def densities(table, prev, own, after, chunks):
    orbs, planes = own.shape[:2]
    return pl.pallas_call(
        density_kernel,
        in_specs=[pl.BlockSpec(memory_space=pltpu.SMEM)] + [pl.BlockSpec(memory_space=pl.ANY)] * 3,
        out_specs=[pl.BlockSpec(memory_space=pltpu.VMEM)] * len(chunks),
        out_shape=[
            jax.ShapeDtypeStruct((count, 2 * planes, BOX, LANES), jnp.float32) for count in chunks
        ],
        scratch_shapes=[
            pltpu.VMEM((3 * orbs, planes, ROWS, LANES), jnp.float32),
            pltpu.SemaphoreType.DMA((3,)),
        ],
        compiler_params=params(),
    )(table, prev, own, after)


def exchange_kernel(table_ref, prev_ref, own_ref, next_ref, *rest):
    pot_refs = rest[:-7]
    before_ref, mid_ref, after_ref, ext, acc, moved, sems = rest[-7:]
    copies = fetch((prev_ref, own_ref, next_ref), ext, sems)
    clear_pads(ext)
    orbs, planes = mid_ref.shape[:2]
    zeros = jnp.zeros((planes, BOX, LANES), jnp.float32)
    low = lane_index((BOX, LANES)) < BOX

    @pl.loop(0, 3 * orbs)
    def _(orb):
        acc[orb] = zeros

    for x in range(planes):
        moved[x, :PAD] = jnp.zeros((PAD, LANES), jnp.float32)
        moved[x, PAD + BOX :] = jnp.zeros((PAD, LANES), jnp.float32)
    for copy in copies:
        copy.wait()

    def add_terms(slot, potential):
        first = table_ref[FIRST, slot]
        second = table_ref[SECOND, slot]
        by_y = table_ref[BY_Y, slot]
        by_z = table_ref[BY_Z, slot]
        weight = table_ref[LIVE, slot].astype(jnp.float32)
        for x in range(planes):
            pot = weight * potential(x)
            partner = moved_z(ext[second, x, pl.ds(PAD - by_y, BOX), :], by_z)
            acc[first, x] += pot * partner
            moved[x, PAD : PAD + BOX] = moved_z(pot * ext[first, x, PAD : PAD + BOX, :], -by_z)
        for x in range(planes):
            acc[second, x] += moved[x, pl.ds(PAD + by_y, BOX), :]

    done = 0
    for pot_ref in pot_refs:
        count = pot_ref.shape[0]

        @pl.loop(0, count)
        def _(pair):
            slot = 2 * (done + pair)
            add_terms(
                slot,
                lambda x: jnp.where(low, pot_ref[pair, x], swapped(pot_ref[pair, planes + x])),
            )
            add_terms(
                slot + 1,
                lambda x: jnp.where(low, swapped(pot_ref[pair, x]), pot_ref[pair, planes + x]),
            )

        done += count

    before_ref[...] = acc[:orbs]
    mid_ref[...] = acc[orbs : 2 * orbs]
    after_ref[...] = acc[2 * orbs :]


def exchange_terms(table, potentials, prev, own, after):
    orbs, planes = own.shape[:2]
    vmem = pl.BlockSpec(memory_space=pltpu.VMEM)
    return pl.pallas_call(
        exchange_kernel,
        in_specs=[pl.BlockSpec(memory_space=pltpu.SMEM)]
        + [pl.BlockSpec(memory_space=pl.ANY)] * 3
        + [vmem] * len(potentials),
        out_specs=[vmem] * 3,
        out_shape=[jax.ShapeDtypeStruct(own.shape, jnp.float32)] * 3,
        scratch_shapes=[
            pltpu.VMEM((3 * orbs, planes, ROWS, LANES), jnp.float32),
            pltpu.VMEM((3 * orbs, planes, BOX, LANES), jnp.float32),
            pltpu.VMEM((planes, ROWS, LANES), jnp.float32),
            pltpu.SemaphoreType.DMA((3,)),
        ],
        compiler_params=params(),
    )(table, prev, own, after, *potentials)


SUB = 8


def coefficients():
    sigma = THETA / DELTA
    coef = 1.0 / sigma
    made = []
    for _ in range(PASSES - 1):
        new = 1.0 / (2.0 * sigma - coef)
        made.append((new * coef, 2.0 * new / (DELTA * DIAG)))
        coef = new
    return made


def solve_kernel(slabs, table_ref, far_ref, own_ref, near_ref, out_ref, dens, even, odd):
    slab = table_ref[SLAB, 0]
    pairs, planes = own_ref.shape[:2]
    flip = lax.rem(slab, 2)
    far_at = flip * 2 * planes
    near_at = (1 - flip) * 2 * planes
    z = lane_index((SUB, SUB, LANES)) & (BOX - 1)
    not_first = z > 0
    not_last = z < BOX - 1
    row = lax.broadcasted_iota(jnp.int32, (SUB, LANES), 0)
    below_in = jnp.where(slab > 0, 1.0, 0.0)
    above_in = jnp.where(slab < slabs - 1, 1.0, 0.0)
    core = slice(1, 1 + SUB)

    def put(buf, x, block):
        buf[x, core] = block
        buf[x, 0] = jnp.where(row > 0, pltpu.roll(block[SUB - 1], 1, 0), 0.0)
        buf[x, 1 + SUB] = jnp.where(row < SUB - 1, pltpu.roll(block[0], SUB - 1, 0), 0.0)

    def take(ref, pair, x):
        return jnp.stack([ref[pair, x, pl.ds(t, SUB, stride=SUB), :] for t in range(SUB)])

    @pl.loop(0, pairs)
    def _(pair):
        for x in range(planes):
            put(dens, far_at + x, take(far_ref, pair, x))
            put(dens, planes + x, take(own_ref, pair, x))
            put(dens, near_at + x, take(near_ref, pair, x))
        start = 1.0 / (DIAG * THETA)
        for turn, (keep, add) in enumerate(coefficients(), 1):
            source = dens if turn == 1 else (even if turn % 2 else odd)
            target = odd if turn % 2 else even
            here = 1.0 + keep - DIAG * add
            for x in range(turn + 1, 3 * planes - 1 - turn):
                mid = source[x, core]
                near = source[x - 1, core] + source[x + 1, core]
                near = near + (source[x, :SUB] + source[x, 2 : 2 + SUB])
                near = near + jnp.where(not_first, pltpu.roll(mid, 1, 2), 0.0)
                near = near + jnp.where(not_last, pltpu.roll(mid, LANES - 1, 2), 0.0)
                if turn == 1:
                    fresh = (here * start + add) * mid + (add * start) * near
                elif turn == 2:
                    fresh = here * mid + (add - keep * start) * dens[x, core] + add * near
                else:
                    fresh = here * mid - keep * target[x, core] + add * (near + dens[x, core])
                if x < planes:
                    fresh = fresh * below_in
                if x >= 2 * planes:
                    fresh = fresh * above_in
                if turn < PASSES - 1:
                    put(target, x, fresh)
                else:
                    for t in range(SUB):
                        out_ref[pair, x - planes, pl.ds(t, SUB, stride=SUB), :] = fresh[t]


def solve(table, far, own, near, slabs):
    planes = own.shape[1]
    vmem = pl.BlockSpec(memory_space=pltpu.VMEM)
    return pl.pallas_call(
        functools.partial(solve_kernel, slabs),
        in_specs=[pl.BlockSpec(memory_space=pltpu.SMEM), vmem, vmem, vmem],
        out_specs=vmem,
        out_shape=jax.ShapeDtypeStruct(own.shape, jnp.float32),
        scratch_shapes=[pltpu.VMEM((3 * planes, SUB + 2, SUB, LANES), jnp.float32)] * 3,
        compiler_params=params(),
    )(table, far, own, near)


def slot_table(offsets, pairs, live, orb_dev):
    total_orbs = offsets.shape[0]
    start = lax.axis_index(("grp", "orb")) * orb_dev - orb_dev
    local = jnp.mod(pairs - start, total_orbs)
    ids = jnp.arange(total_orbs, dtype=jnp.int32)
    pick_first = (pairs[:, 0:1] == ids[None, :]).astype(jnp.int32)
    pick_second = (pairs[:, 1:2] == ids[None, :]).astype(jnp.int32)
    shift = jnp.sum((pick_second - pick_first)[:, :, None] * offsets[None, :, :], axis=1)
    slab = jnp.broadcast_to(lax.axis_index("slab").astype(jnp.int32), (1, pairs.shape[0]))
    return jnp.concatenate([local.T, shift.T, live[None, :], slab], axis=0)


def solved_terms(count, table, prev, own, after):
    slabs = lax.axis_size("slab")
    across = [(s, s ^ 1) for s in range(slabs)]
    onward = [(s, s + 2 - 4 * (s % 2)) for s in range(slabs)]
    onward = [(s, t) for s, t in onward if 0 <= t < slabs]
    chunks = [count] if count == 1 else [count - count // 2, count // 2]
    made = densities(table, prev, own, after, chunks)
    near = [lax.ppermute(dens, "slab", across) for dens in made]
    far = [lax.ppermute(dens, "slab", onward) for dens in near]
    potentials = [solve(table, f, d, n, slabs) for f, d, n in zip(far, made, near)]
    return exchange_terms(table, potentials, prev, own, after)


def body(orbitals, offsets, pairs, live):
    ring = ("grp", "orb")
    table = slot_table(offsets, pairs, live, orbitals.shape[0])
    own = pack(orbitals)
    prev = shifted(own, ring, 1)
    after = shifted(own, ring, -1)
    most = (live.shape[0] + 1) // 2
    count = jnp.clip((jnp.sum(live) + 1) // 2, 1, most)
    to_prior, middle, to_next = lax.switch(
        count - 1,
        [functools.partial(solved_terms, k) for k in range(1, most + 1)],
        table,
        prev,
        own,
        after,
    )
    return finish(middle, shifted(to_prior, ring, -1), shifted(to_next, ring, 1))


def solution(mesh):
    placed = (
        P(("grp", "orb"), "slab", None, None),
        P(),
        P(("grp", "orb"), None),
        P(("grp", "orb")),
    )
    return jax.shard_map(
        body,
        mesh=mesh,
        in_specs=placed,
        out_specs=P(("grp", "orb"), "slab", None, None),
        check_vma=False,
    )
```

time: 150 us -> 131 us (0.87)
  the two profiles are of different devices: /device:TPU:2 before, /device:TPU:134 now
where the time goes in v2:
time: 131 us
  waiting for transfers between devices  60.6 us (46%)
  starting transfers between devices  56 us (43%)
  Pallas kernels  10.3 us (8%)
  local copies, waits for them, and re-layouts  1.68 us (1%)
    ppermute x4, starting transfers between devices, shifted(): lax.ppermute(shard, axis, [(i, (i + by) % size) for i in range(size)])  48.9 us
    ppermute x4, waiting for transfers between devices, shifted(): lax.ppermute(shard, axis, [(i, (i + by) % size) for i in range(size)])  44.4 us
    ppermute x1, waiting for transfers between devices, solved_terms(): far = [lax.ppermute(dens, 'slab', onward) for dens in near]  8.26 us
    ppermute x1, waiting for transfers between devices, solved_terms(): near = [lax.ppermute(dens, 'slab', across) for dens in made]  8.03 us
    ppermute x1, starting transfers between devices, solved_terms(): near = [lax.ppermute(dens, 'slab', across) for dens in made]  5.81 us
    pallas_call x1, Pallas kernels, exchange_terms(): pl.pallas_call(exchange_kernel, in_specs=[pl.BlockSpec(memory_space=pltpu...  3.46 us
  transfers between devices with their start and end apart: 6, of which 6 were waited for; matrix products, arithmetic and copies ran while one was open for 1% of the time, Pallas kernels for 0%

profile of v2, /device:TPU:134, one launch (start us, length us, event | category | flops | bytes accessed | tf_op | source)
XLA Modules:
  0.0 130.6 jit_solution(8099010787970726436)
XLA Ops:
  0.0 0.0 copy-start
  0.0 1.6 %copy-done = f32[8,8,64,64]{3,2,1,0:T(8,128)S(1)} copy-done((f32[8,8,64,64]{3,2,1,0:T(8,128)S(1)}, f32[8,8,64,64]{3,2,1,0:T(8,128)}, u32[]{:S(2)}) %copy-start) | copy-done | bytes 1048600
  1.6 0.0 copy-start.3
  1.6 0.0 copy-start.1
  1.6 0.0 copy-start.2
  1.6 0.4 shard_map.46
  2.0 4.0 %collective-permute-start.15 = (f32[8,4,64,128]{3,2,1,0:T(8,128)S(1)}, f32[8,4,64,128]{3,2,1,0:T(8,128)S(1)}, u32[]{:S(2)}, u32[]{:S(2)}) collective-permute-start(f32[8,4,64,128]{3,2,1,0:T(8,128)S(1)} %shard_map.46), channel_id=1, source_target_pairs={{0,504},{8,0},{16,8},{24,16},{32,24},{40,32},{48,40},{56,48},{64,5... | collective-permute-start | bytes 3145736 | tf_op jit(solution)/shard_map/ppermute | solution.py:28
  6.1 1.9 %collective-permute-start.14 = (f32[8,4,64,128]{3,2,1,0:T(8,128)S(1)}, f32[8,4,64,128]{3,2,1,0:T(8,128)S(1)}, u32[]{:S(2)}, u32[]{:S(2)}) collective-permute-start(f32[8,4,64,128]{3,2,1,0:T(8,128)S(1)} %shard_map.46), channel_id=1, source_target_pairs={{0,8},{8,16},{16,24},{24,32},{32,40},{40,48},{48,56},{56,64},{64,7... | collective-permute-start | bytes 3145736 | tf_op jit(solution)/shard_map/ppermute | solution.py:28
  8.0 0.0 copy-done.3
  8.0 0.6 reduce_sum.18
  9.3 0.1 pad.3.clone
  9.4 0.0 copy-done.1
  9.4 0.1 convert_subtract_fusion
  9.5 0.0 copy-done.2
  9.5 0.1 multiply_reduce_fusion
  9.7 0.1 add_add_fusion
  9.7 19.1 %collective-permute-done.15 = f32[8,4,64,128]{3,2,1,0:T(8,128)S(1)} collective-permute-done((f32[8,4,64,128]{3,2,1,0:T(8,128)S(1)}, f32[8,4,64,128]{3,2,1,0:T(8,128)S(1)}, u32[]{:S(2)}, u32[]{:S(2)}) %collective-permute-start.15) | collective-permute-done | bytes 1048608 | tf_op jit(solution)/shard_map/ppermute | solution.py:28
  28.8 1.8 %collective-permute-done.14 = f32[8,4,64,128]{3,2,1,0:T(8,128)S(1)} collective-permute-done((f32[8,4,64,128]{3,2,1,0:T(8,128)S(1)}, f32[8,4,64,128]{3,2,1,0:T(8,128)S(1)}, u32[]{:S(2)}, u32[]{:S(2)}) %collective-permute-start.14) | collective-permute-done | bytes 1048608 | tf_op jit(solution)/shard_map/ppermute | solution.py:28
  30.6 31.0 %conditional.1 = ((f32[8,4,64,128]{3,2,1,0:T(8,128)}, f32[8,4,64,128]{3,2,1,0:T(8,128)}, f32[8,4,64,128]{3,2,1,0:T(8,128)})) conditional(s32[]{:T(128)} %clamp.3, (s32[6,8]{1,0:T(8,128)S(1)}, f32[8,4,64,128]{3,2,1,0:T(8,128)S(1)}, f32[8,4,64,128]{3,2,1,0:T(8,128)S(1)}, f32[8,4,64,128]{3,2,1,0:T(8,128)S(1)}) %tuple.17, ...), branch_computations={%region_2.3_spmd, %region_3.4_spmd, %region_4.5_spmd, %region_5.6_... | conditional | bytes 8388776 | solution.py:349
  30.6 1.3 %branch_0_fun.3.own_ref = f32[1,8,64,128]{3,2,1,0:T(8,128)S(1)} custom-call(s32[6,8]{1,0:T(8,128)S(1)} %get-tuple-element.37.table_ref, f32[8,4,64,128]{3,2,1,0:T(8,128)S(1)} %get-tuple-element.38.prev_ref, f32[8,4,64,128]{3,2,1,0:T(8,128)S(1)} %get-tuple-element.39.own_ref, f32[8,4,64,128]{3,2,1,0:T(8,128)S(1)} %get-tuple-element.40.next_ref), custom_call_target="tpu_custom_call" | custom-call | tf_op jit(solution)/shard_map/cond/branch_0_fun/pallas_call | solution.py:142
  32.0 5.8 %collective-permute-start = (f32[1,8,64,128]{3,2,1,0:T(8,128)S(1)}, f32[1,8,64,128]{3,2,1,0:T(8,128)S(1)}, u32[]{:S(2)}, u32[]{:S(2)}) collective-permute-start(f32[1,8,64,128]{3,2,1,0:T(8,128)S(1)} %branch_0_fun.3.own_ref), channel_id=1, source_target_pairs={{0,1},{1,0},{2,3},{3,2},{4,5},{5,4},{6,7},{7,6},{8,9},{9,8},{10,11... | collective-permute-start | bytes 786440 | tf_op jit(solution)/shard_map/cond/branch_0_fun/ppermute | solution.py:335
  37.8 8.0 %collective-permute-done.near_ref = f32[1,8,64,128]{3,2,1,0:T(8,128)S(1)} collective-permute-done((f32[1,8,64,128]{3,2,1,0:T(8,128)S(1)}, f32[1,8,64,128]{3,2,1,0:T(8,128)S(1)}, u32[]{:S(2)}, u32[]{:S(2)}) %collective-permute-start) | collective-permute-done | bytes 262176 | tf_op jit(solution)/shard_map/cond/branch_0_fun/ppermute | solution.py:335
  45.8 1.3 collective-permute-start.1
  47.1 8.3 %collective-permute-done.1.far_ref = f32[1,8,64,128]{3,2,1,0:T(8,128)S(1)} collective-permute-done((f32[1,8,64,128]{3,2,1,0:T(8,128)S(1)}, f32[1,8,64,128]{3,2,1,0:T(8,128)S(1)}, u32[]{:S(2)}, u32[]{:S(2)}) %collective-permute-start.1) | collective-permute-done | bytes 262176 | tf_op jit(solution)/shard_map/cond/branch_0_fun/ppermute | solution.py:336
  55.4 2.6 %branch_0_fun.4.rest_0_ = f32[1,8,64,128]{3,2,1,0:T(8,128)S(1)} custom-call(s32[6,8]{1,0:T(8,128)S(1)} %get-tuple-element.37.table_ref, f32[1,8,64,128]{3,2,1,0:T(8,128)S(1)} %collective-permute-done.1.far_ref, f32[1,8,64,128]{3,2,1,0:T(8,128)S(1)} %branch_0_fun.3.own_ref, f32[1,8,64,128]{3,2,1,0:T(8,128)S(1)} %collective-permute-done.near_ref), custom_call_target="tpu_custom_call" | custom-call | tf_op jit(solution)/shard_map/cond/branch_0_fun/pallas_call | solution.py:306
  57.9 3.5 %branch_0_fun.5 = (f32[8,4,64,128]{3,2,1,0:T(8,128)}, f32[8,4,64,128]{3,2,1,0:T(8,128)}, f32[8,4,64,128]{3,2,1,0:T(8,128)}) custom-call(s32[6,8]{1,0:T(8,128)S(1)} %get-tuple-element.37.table_ref, f32[8,4,64,128]{3,2,1,0:T(8,128)S(1)} %get-tuple-element.38.prev_ref, f32[8,4,64,128]{3,2,1,0:T(8,128)S(1)} %get-tuple-element.39.own_ref, ...), custom_call_target="tpu_custom_call" | custom-call | tf_op jit(solution)/shard_map/cond/branch_0_fun/pallas_call | solution.py:216
  61.6 41.0 %collective-permute-start.16 = (f32[8,4,64,128]{3,2,1,0:T(8,128)}, f32[8,4,64,128]{3,2,1,0:T(8,128)S(1)}, u32[]{:S(2)}, u32[]{:S(2)}) collective-permute-start(f32[8,4,64,128]{3,2,1,0:T(8,128)} %get-tuple-element.63), channel_id=1, source_target_pairs={{0,504},{8,0},{16,8},{24,16},{32,24},{40,32},{48,40},{56,48},{64,5... | collective-permute-start | bytes 3145736 | tf_op jit(solution)/shard_map/ppermute | solution.py:28
  102.6 1.9 %collective-permute-start.17 = (f32[8,4,64,128]{3,2,1,0:T(8,128)}, f32[8,4,64,128]{3,2,1,0:T(8,128)S(1)}, u32[]{:S(2)}, u32[]{:S(2)}) collective-permute-start(f32[8,4,64,128]{3,2,1,0:T(8,128)} %get-tuple-element.64), channel_id=1, source_target_pairs={{0,8},{8,16},{16,24},{24,32},{32,40},{40,48},{48,56},{56,64},{64,7... | collective-permute-start | bytes 3145736 | tf_op jit(solution)/shard_map/ppermute | solution.py:28
  104.6 10.7 %collective-permute-done.16.next_ref = f32[8,4,64,128]{3,2,1,0:T(8,128)S(1)} collective-permute-done((f32[8,4,64,128]{3,2,1,0:T(8,128)}, f32[8,4,64,128]{3,2,1,0:T(8,128)S(1)}, u32[]{:S(2)}, u32[]{:S(2)}) %collective-permute-start.16) | collective-permute-done | bytes 1048608 | tf_op jit(solution)/shard_map/ppermute | solution.py:28
  115.2 12.8 %collective-permute-done.17.prior_ref = f32[8,4,64,128]{3,2,1,0:T(8,128)S(1)} collective-permute-done((f32[8,4,64,128]{3,2,1,0:T(8,128)}, f32[8,4,64,128]{3,2,1,0:T(8,128)S(1)}, u32[]{:S(2)}, u32[]{:S(2)}) %collective-permute-start.17) | collective-permute-done | bytes 1048608 | tf_op jit(solution)/shard_map/ppermute | solution.py:28
  128.0 2.6 %shard_map.47 = f32[8,8,64,64]{3,2,1,0:T(8,128)} custom-call(f32[8,4,64,128]{3,2,1,0:T(8,128)} %get-tuple-element.62.mid_ref, f32[8,4,64,128]{3,2,1,0:T(8,128)S(1)} %collective-permute-done.16.next_ref, f32[8,4,64,128]{3,2,1,0:T(8,128)S(1)} %collective-permute-done.17.prior_ref), custom_call_target="tpu_custom_call" | custom-call | tf_op jit(solution)/shard_map/pallas_call | solution.py:69
  (2 shorter events, 0.0 us)
Async XLA Ops:
  0.0 1.6 %copy-start = (f32[8,8,64,64]{3,2,1,0:T(8,128)S(1)}, f32[8,8,64,64]{3,2,1,0:T(8,128)}, u32[]{:S(2)}) copy-start(f32[8,8,64,64]{3,2,1,0:T(8,128)} %field_ref.1) | copy-start | bytes 3145732
  1.6 6.4 %copy-start.3 = (s32[8]{0:T(128)S(1)}, s32[8]{0:T(128)}, u32[]{:S(2)}) copy-start(s32[8]{0:T(128)} %param.11) | copy-start | bytes 100
  1.6 7.8 %copy-start.1 = (s32[8,2]{0,1:T(2,128)S(1)}, s32[8,2]{0,1:T(2,128)}, u32[]{:S(2)}) copy-start(s32[8,2]{0,1:T(2,128)} %param.10) | copy-start | bytes 196
  1.6 7.9 %copy-start.2 = (s32[512,2]{0,1:T(2,128)S(1)}, s32[512,2]{0,1:T(2,128)}, u32[]{:S(2)}) copy-start(s32[512,2]{0,1:T(2,128)} %param.9) | copy-start | bytes 12292
  2.0 26.8 %collective-permute-start.15 = (f32[8,4,64,128]{3,2,1,0:T(8,128)S(1)}, f32[8,4,64,128]{3,2,1,0:T(8,128)S(1)}, u32[]{:S(2)}, u32[]{:S(2)}) collective-permute-start(f32[8,4,64,128]{3,2,1,0:T(8,128)S(1)} %shard_map.46), channel_id=1, source_target_pairs={{0,504},{8,0},{16,8},{24,16},{32,24},{40,32},{48,40},{56,48},{64,5... | collective-permute-start | bytes 3145736 | tf_op jit(solution)/shard_map/ppermute | solution.py:28
  6.1 24.6 %collective-permute-start.14 = (f32[8,4,64,128]{3,2,1,0:T(8,128)S(1)}, f32[8,4,64,128]{3,2,1,0:T(8,128)S(1)}, u32[]{:S(2)}, u32[]{:S(2)}) collective-permute-start(f32[8,4,64,128]{3,2,1,0:T(8,128)S(1)} %shard_map.46), channel_id=1, source_target_pairs={{0,8},{8,16},{16,24},{24,32},{32,40},{40,48},{48,56},{56,64},{64,7... | collective-permute-start | bytes 3145736 | tf_op jit(solution)/shard_map/ppermute | solution.py:28
  32.0 13.8 %collective-permute-start = (f32[1,8,64,128]{3,2,1,0:T(8,128)S(1)}, f32[1,8,64,128]{3,2,1,0:T(8,128)S(1)}, u32[]{:S(2)}, u32[]{:S(2)}) collective-permute-start(f32[1,8,64,128]{3,2,1,0:T(8,128)S(1)} %branch_0_fun.3.own_ref), channel_id=1, source_target_pairs={{0,1},{1,0},{2,3},{3,2},{4,5},{5,4},{6,7},{7,6},{8,9},{9,8},{10,11... | collective-permute-start | bytes 786440 | tf_op jit(solution)/shard_map/cond/branch_0_fun/ppermute | solution.py:335
  45.8 9.6 %collective-permute-start.1 = (f32[1,8,64,128]{3,2,1,0:T(8,128)S(1)}, f32[1,8,64,128]{3,2,1,0:T(8,128)S(1)}, u32[]{:S(2)}, u32[]{:S(2)}) collective-permute-start(f32[1,8,64,128]{3,2,1,0:T(8,128)S(1)} %collective-permute-done.near_ref), channel_id=1, source_target_pairs={{0,2},{2,4},{3,1},{4,6},{5,3},{7,5},{8,10},{10,12},{11,9},{12,14},... | collective-permute-start | bytes 786440 | tf_op jit(solution)/shard_map/cond/branch_0_fun/ppermute | solution.py:336
  61.6 53.6 %collective-permute-start.16 = (f32[8,4,64,128]{3,2,1,0:T(8,128)}, f32[8,4,64,128]{3,2,1,0:T(8,128)S(1)}, u32[]{:S(2)}, u32[]{:S(2)}) collective-permute-start(f32[8,4,64,128]{3,2,1,0:T(8,128)} %get-tuple-element.63), channel_id=1, source_target_pairs={{0,504},{8,0},{16,8},{24,16},{32,24},{40,32},{48,40},{56,48},{64,5... | collective-permute-start | bytes 3145736 | tf_op jit(solution)/shard_map/ppermute | solution.py:28
  102.6 25.4 %collective-permute-start.17 = (f32[8,4,64,128]{3,2,1,0:T(8,128)}, f32[8,4,64,128]{3,2,1,0:T(8,128)S(1)}, u32[]{:S(2)}, u32[]{:S(2)}) collective-permute-start(f32[8,4,64,128]{3,2,1,0:T(8,128)} %get-tuple-element.64), channel_id=1, source_target_pairs={{0,8},{8,16},{16,24},{24,32},{32,40},{40,48},{48,56},{56,64},{64,7... | collective-permute-start | bytes 3145736 | tf_op jit(solution)/shard_map/ppermute | solution.py:28

commit v3 on v2

--- a/solution.py
+++ b/solution.py
@@ -23,9 +23,16 @@
     return pltpu.CompilerParams(vmem_limit_bytes=VMEM_BYTES)
 
 
-def shifted(shard, axis, by):
-    size = lax.axis_size(axis)
-    return lax.ppermute(shard, axis, [(i, (i + by) % size) for i in range(size)])
+RING = ("grp", "orb")
+
+
+def even_edges():
+    return [(g, g ^ 1) for g in range(lax.axis_size(RING))]
+
+
+def odd_edges():
+    size = lax.axis_size(RING)
+    return [(g, (g + 1 if g % 2 else g - 1) % size) for g in range(size)]
 
 
 def lane_index(shape):
@@ -56,27 +63,116 @@
     )(orbitals)
 
 
-def finish_kernel(mid_ref, next_ref, prior_ref, out_ref):
-    half = mid_ref.shape[1]
-    total = mid_ref[...] + next_ref[...] + prior_ref[...]
-    out_ref[:, :half] = total[..., :BOX]
-    out_ref[:, half:] = total[..., BOX:]
-
-
-def finish(middle, from_next, from_prior):
+def finish_kernel(table_ref, asked_ref, mid_ref, pal_ref, far_ref, out_ref, acc):
+    orbs, half = mid_ref.shape[:2]
+    acc[...] = mid_ref[...] + pal_ref[...]
+    rank = 0
+    for slot in range(asked_ref.shape[0]):
+        local = asked_ref[slot] - orbs * table_ref[GROUP, 0]
+        hit = (local >= 0) & (local < orbs)
+        if slot:
+            rank = jnp.minimum(rank, far_ref.shape[0] - 1)
+
+        @pl.when(hit)
+        def _():
+            acc[local] += far_ref[rank]
+
+        rank += hit.astype(jnp.int32)
+    out_ref[:, :half] = acc[..., :BOX]
+    out_ref[:, half:] = acc[..., BOX:]
+
+
+def finish(table, asked, middle, from_pal, from_far):
     orbs, half = middle.shape[:2]
-    spec = pl.BlockSpec((orbs // 2, half, BOX, LANES), lambda i: (i, 0, 0, 0))
+    smem = pl.BlockSpec(memory_space=pltpu.SMEM)
+    vmem = pl.BlockSpec(memory_space=pltpu.VMEM)
     return pl.pallas_call(
         finish_kernel,
-        grid=(2,),
-        in_specs=[spec] * 3,
-        out_specs=pl.BlockSpec((orbs // 2, 2 * half, BOX, BOX), lambda i: (i, 0, 0, 0)),
+        in_specs=[smem, smem, vmem, vmem, vmem],
+        out_specs=vmem,
         out_shape=jax.ShapeDtypeStruct((orbs, 2 * half, BOX, BOX), jnp.float32),
-        compiler_params=params(),
-    )(middle, from_next, from_prior)
-
-
-FIRST, SECOND, BY_Y, BY_Z, LIVE, SLAB = range(6)
+        scratch_shapes=[pltpu.VMEM(middle.shape, jnp.float32)],
+        compiler_params=params(),
+    )(table, asked, middle, from_pal, from_far)
+
+
+def gather_kernel(table_ref, asked_ref, own_ref, out_ref, sems):
+    orbs, count = own_ref.shape[0], out_ref.shape[0]
+    chosen = [0] * count
+    rank = 0
+    for slot in range(asked_ref.shape[0]):
+        local = asked_ref[slot] - orbs * table_ref[GROUP, 0]
+        hit = (local >= 0) & (local < orbs)
+        chosen = [jnp.where(hit & (rank == k), local, old) for k, old in enumerate(chosen)]
+        rank += hit.astype(jnp.int32)
+    copies = [
+        pltpu.make_async_copy(own_ref.at[orb], out_ref.at[k], sems.at[k])
+        for k, orb in enumerate(chosen)
+    ]
+    for copy in copies:
+        copy.start()
+    for copy in copies:
+        copy.wait()
+
+
+def gather(table, asked, own, count):
+    smem = pl.BlockSpec(memory_space=pltpu.SMEM)
+    anywhere = pl.BlockSpec(memory_space=pl.ANY)
+    return pl.pallas_call(
+        gather_kernel,
+        in_specs=[smem, smem, anywhere],
+        out_specs=anywhere,
+        out_shape=jax.ShapeDtypeStruct((count,) + own.shape[1:], jnp.float32),
+        scratch_shapes=[pltpu.SemaphoreType.DMA((count,))],
+        compiler_params=params(),
+    )(table, asked, own)
+
+
+def spread_kernel(in_ref, out_ref, sem):
+    copy = pltpu.make_async_copy(in_ref, out_ref.at[pl.ds(0, in_ref.shape[0])], sem)
+    copy.start()
+    copy.wait()
+
+
+def spread(blocks, count):
+    if blocks.shape[0] == count:
+        return blocks
+    anywhere = pl.BlockSpec(memory_space=pl.ANY)
+    return pl.pallas_call(
+        spread_kernel,
+        in_specs=[anywhere],
+        out_specs=anywhere,
+        out_shape=jax.ShapeDtypeStruct((count,) + blocks.shape[1:], jnp.float32),
+        scratch_shapes=[pltpu.SemaphoreType.DMA],
+        compiler_params=params(),
+    )(blocks)
+
+
+def ask(count, most, table, asked, own):
+    return spread(lax.ppermute(gather(table, asked, own, count), RING, odd_edges()), most)
+
+
+def answer(count, most, terms):
+    return spread(lax.ppermute(terms[:count], RING, odd_edges()), most)
+
+
+FIRST, SECOND, BY_Y, BY_Z, GROUP, SLAB = range(6)
+
+
+def locate(table_ref, where_ref, orbs):
+    group = table_ref[GROUP, 0]
+    pal = group ^ 1
+    rank = 0
+    for slot in range(where_ref.shape[0]):
+        second = table_ref[SECOND, slot]
+        mine = second - orbs * group
+        other = second - orbs * pal
+        is_mine = (mine >= 0) & (mine < orbs)
+        is_pal = (other >= 0) & (other < orbs)
+        is_far = (second >= 0) & ~is_mine & ~is_pal
+        place = jnp.where(is_pal, orbs + other, jnp.where(is_far, 2 * orbs + rank, 0))
+        where_ref[slot] = jnp.where(is_mine, mine, place)
+        rank += is_far.astype(jnp.int32)
 
 
 def clear_pads(ext):
@@ -90,13 +186,12 @@
 
 def fetch(refs, ext, sems):
     copies = []
+    done = 0
     for k, ref in enumerate(refs):
         orbs = ref.shape[0]
-        copies.append(
-            pltpu.make_async_copy(
-                ref, ext.at[pl.ds(k * orbs, orbs), :, pl.ds(PAD, BOX), :], sems.at[k]
-            )
-        )
+        target = ext.at[pl.ds(done, orbs), :, pl.ds(PAD, BOX), :]
+        copies.append(pltpu.make_async_copy(ref, target, sems.at[k]))
+        done += orbs
     for copy in copies:
         copy.start()
     return copies
@@ -106,10 +201,11 @@
     return pltpu.roll(field, LANES // 2, 1)
 
 
-def density_kernel(table_ref, prev_ref, own_ref, next_ref, *rest):
-    out_refs, ext, sems = rest[:-2], rest[-2], rest[-1]
-    copies = fetch((prev_ref, own_ref, next_ref), ext, sems)
+def density_kernel(table_ref, own_ref, pal_ref, far_ref, *rest):
+    out_refs, (ext, where, sems) = rest[:-3], rest[-3:]
+    copies = fetch((own_ref, pal_ref, far_ref), ext, sems)
     clear_pads(ext)
+    locate(table_ref, where, own_ref.shape[0])
     for copy in copies:
         copy.wait()
     planes = own_ref.shape[1]
@@ -117,7 +213,7 @@
 
     def density(slot, x):
         first = table_ref[FIRST, slot]
-        second = table_ref[SECOND, slot]
+        second = where[slot]
         partner = ext[second, x, pl.ds(PAD - table_ref[BY_Y, slot], BOX), :]
         return ext[first, x, PAD : PAD + BOX, :] * moved_z(partner, table_ref[BY_Z, slot])
 
@@ -137,7 +233,7 @@
         done += count
 
 
-def densities(table, prev, own, after, chunks):
+def densities(table, own, pal, far, chunks):
     orbs, planes = own.shape[:2]
     return pl.pallas_call(
         density_kernel,
@@ -147,23 +243,25 @@
             jax.ShapeDtypeStruct((count, 2 * planes, BOX, LANES), jnp.float32) for count in chunks
         ],
         scratch_shapes=[
-            pltpu.VMEM((3 * orbs, planes, ROWS, LANES), jnp.float32),
+            pltpu.VMEM((2 * orbs + far.shape[0], planes, ROWS, LANES), jnp.float32),
+            pltpu.SMEM((table.shape[1],), jnp.int32),
             pltpu.SemaphoreType.DMA((3,)),
         ],
         compiler_params=params(),
-    )(table, prev, own, after)
-
-
-def exchange_kernel(table_ref, prev_ref, own_ref, next_ref, *rest):
-    pot_refs = rest[:-7]
-    before_ref, mid_ref, after_ref, ext, acc, moved, sems = rest[-7:]
-    copies = fetch((prev_ref, own_ref, next_ref), ext, sems)
+    )(table, own, pal, far)
+
+
+def exchange_kernel(table_ref, own_ref, pal_ref, far_ref, *rest):
+    pot_refs = rest[:-8]
+    mid_ref, to_pal_ref, to_far_ref, ext, acc, moved, where, sems = rest[-8:]
+    copies = fetch((own_ref, pal_ref, far_ref), ext, sems)
     clear_pads(ext)
+    locate(table_ref, where, own_ref.shape[0])
     orbs, planes = mid_ref.shape[:2]
     zeros = jnp.zeros((planes, BOX, LANES), jnp.float32)
     low = lane_index((BOX, LANES)) < BOX
 
-    @pl.loop(0, 3 * orbs)
+    @pl.loop(0, acc.shape[0])
     def _(orb):
         acc[orb] = zeros
 
@@ -175,10 +273,10 @@
 
     def add_terms(slot, potential):
         first = table_ref[FIRST, slot]
-        second = table_ref[SECOND, slot]
+        second = where[slot]
         by_y = table_ref[BY_Y, slot]
         by_z = table_ref[BY_Z, slot]
-        weight = table_ref[LIVE, slot].astype(jnp.float32)
+        weight = jnp.where(table_ref[SECOND, slot] >= 0, 1.0, 0.0)
         for x in range(planes):
             pot = weight * potential(x)
             partner = moved_z(ext[second, x, pl.ds(PAD - by_y, BOX), :], by_z)
@@ -205,12 +303,12 @@
 
         done += count
 
-    before_ref[...] = acc[:orbs]
-    mid_ref[...] = acc[orbs : 2 * orbs]
-    after_ref[...] = acc[2 * orbs :]
-
-
-def exchange_terms(table, potentials, prev, own, after):
+    mid_ref[...] = acc[:orbs]
+    to_pal_ref[...] = acc[orbs : 2 * orbs]
+    to_far_ref[...] = acc[2 * orbs :]
+
+
+def exchange_terms(table, potentials, own, pal, far):
     orbs, planes = own.shape[:2]
     vmem = pl.BlockSpec(memory_space=pltpu.VMEM)
     return pl.pallas_call(
@@ -219,15 +317,16 @@
         + [pl.BlockSpec(memory_space=pl.ANY)] * 3
         + [vmem] * len(potentials),
         out_specs=[vmem] * 3,
-        out_shape=[jax.ShapeDtypeStruct(own.shape, jnp.float32)] * 3,
+        out_shape=[jax.ShapeDtypeStruct(a.shape, jnp.float32) for a in (own, pal, far)],
         scratch_shapes=[
-            pltpu.VMEM((3 * orbs, planes, ROWS, LANES), jnp.float32),
-            pltpu.VMEM((3 * orbs, planes, BOX, LANES), jnp.float32),
+            pltpu.VMEM((2 * orbs + far.shape[0], planes, ROWS, LANES), jnp.float32),
+            pltpu.VMEM((2 * orbs + far.shape[0], planes, BOX, LANES), jnp.float32),
             pltpu.VMEM((planes, ROWS, LANES), jnp.float32),
+            pltpu.SMEM((table.shape[1],), jnp.int32),
             pltpu.SemaphoreType.DMA((3,)),
         ],
         compiler_params=params(),
-    )(table, prev, own, after, *potentials)
+    )(table, own, pal, far, *potentials)
 
 
 SUB = 8
@@ -313,48 +412,69 @@
     )(table, far, own, near)
 
 
-def slot_table(offsets, pairs, live, orb_dev):
+def slot_table(offsets, pairs, seconds, orb_dev):
     total_orbs = offsets.shape[0]
-    start = lax.axis_index(("grp", "orb")) * orb_dev - orb_dev
-    local = jnp.mod(pairs - start, total_orbs)
+    group = lax.axis_index(RING).astype(jnp.int32)
     ids = jnp.arange(total_orbs, dtype=jnp.int32)
     pick_first = (pairs[:, 0:1] == ids[None, :]).astype(jnp.int32)
     pick_second = (pairs[:, 1:2] == ids[None, :]).astype(jnp.int32)
     shift = jnp.sum((pick_second - pick_first)[:, :, None] * offsets[None, :, :], axis=1)
-    slab = jnp.broadcast_to(lax.axis_index("slab").astype(jnp.int32), (1, pairs.shape[0]))
-    return jnp.concatenate([local.T, shift.T, live[None, :], slab], axis=0)
-
-
-def solved_terms(count, table, prev, own, after):
+    constants = jnp.stack([group, lax.axis_index("slab").astype(jnp.int32)])
+    return jnp.concatenate(
+        [
+            (pairs[:, 0] - orb_dev * group)[None, :],
+            seconds[None, :],
+            shift.T,
+            jnp.broadcast_to(constants[:, None], (2, pairs.shape[0])),
+        ],
+        axis=0,
+    )
+
+
+def asked_by(seconds, group, orb_dev):
+    local = seconds - orb_dev * group
+    return jnp.sum(((local >= 0) & (local < orb_dev)).astype(jnp.int32))
+
+
+def solved_terms(count, table, own, pal, far):
     slabs = lax.axis_size("slab")
     across = [(s, s ^ 1) for s in range(slabs)]
     onward = [(s, s + 2 - 4 * (s % 2)) for s in range(slabs)]
     onward = [(s, t) for s, t in onward if 0 <= t < slabs]
     chunks = [count] if count == 1 else [count - count // 2, count // 2]
-    made = densities(table, prev, own, after, chunks)
+    made = densities(table, own, pal, far, chunks)
     near = [lax.ppermute(dens, "slab", across) for dens in made]
-    far = [lax.ppermute(dens, "slab", onward) for dens in near]
-    potentials = [solve(table, f, d, n, slabs) for f, d, n in zip(far, made, near)]
-    return exchange_terms(table, potentials, prev, own, after)
+    next_but_one = [lax.ppermute(dens, "slab", onward) for dens in near]
+    potentials = [solve(table, f, d, n, slabs) for f, d, n in zip(next_but_one, made, near)]
+    return exchange_terms(table, potentials, own, pal, far)
 
 
 def body(orbitals, offsets, pairs, live):
-    ring = ("grp", "orb")
-    table = slot_table(offsets, pairs, live, orbitals.shape[0])
+    orbs, slots = orbitals.shape[0], live.shape[0]
+    seconds = jnp.where(live > 0, pairs[:, 1], -1)
+    asked = lax.ppermute(seconds, RING, odd_edges())
     own = pack(orbitals)
-    prev = shifted(own, ring, 1)
-    after = shifted(own, ring, -1)
-    most = (live.shape[0] + 1) // 2
-    count = jnp.clip((jnp.sum(live) + 1) // 2, 1, most)
-    to_prior, middle, to_next = lax.switch(
-        count - 1,
-        [functools.partial(solved_terms, k) for k in range(1, most + 1)],
-        table,
-        prev,
-        own,
-        after,
-    )
-    return finish(middle, shifted(to_prior, ring, -1), shifted(to_next, ring, 1))
+    pal = lax.ppermute(own, RING, even_edges())
+    table = slot_table(offsets, pairs, seconds, orbs)
+
+    group = lax.axis_index(RING)
+    beyond = (group + 2 * (group % 2) - 1) % lax.axis_size(RING)
+    most = slots - 1
+    longer = jnp.maximum(asked_by(asked, group, orbs), asked_by(seconds, beyond, orbs))
+    length = jnp.clip(longer, 1, most) - 1
+    lengths = range(1, most + 1)
+    asks = [functools.partial(ask, k, most) for k in lengths]
+    far = lax.switch(length, asks, table, asked, own)
+
+    pairs_most = (slots + 1) // 2
+    count = jnp.clip((jnp.sum(live) + 1) // 2, 1, pairs_most)
+    solves = [functools.partial(solved_terms, k) for k in range(1, pairs_most + 1)]
+    middle, to_pal, to_far = lax.switch(count - 1, solves, table, own, pal, far)
+
+    from_pal = lax.ppermute(to_pal, RING, even_edges())
+    answers = [functools.partial(answer, k, most) for k in lengths]
+    from_far = lax.switch(length, answers, to_far)
+    return finish(table, asked, middle, from_pal, from_far)
 
 
 def solution(mesh):

time: 131 us -> 108 us (0.82)
  the two profiles are of different devices: /device:TPU:134 before, /device:TPU:71 now
where the time goes in v3:
time: 108 us
  waiting for transfers between devices  50.8 us (47%)
  starting transfers between devices  29.8 us (28%)
  Pallas kernels  21.2 us (20%)
  between operations  1.96 us (2%)
  local copies, waits for them, and re-layouts  1.71 us (2%)
  other arithmetic  1.67 us (2%)
    ppermute x2, waiting for transfers between devices, solved_terms(): near = [lax.ppermute(dens, 'slab', across) for dens in made]  27.2 us
    ppermute x2, waiting for transfers between devices, solved_terms(): next_but_one = [lax.ppermute(dens, 'slab', onward) for dens in near]  9.69 us
    ppermute x2, starting transfers between devices, solved_terms(): near = [lax.ppermute(dens, 'slab', across) for dens in made]  9.37 us
    ppermute x1, waiting for transfers between devices, answer(): return spread(lax.ppermute(terms[:count], RING, odd_edges()), most)  7.17 us
    pallas_call x2, Pallas kernels, solve(): pl.pallas_call(functools.partial(solve_kernel, slabs), in_specs=[pl.Block...  7.15 us
    ppermute x1, starting transfers between devices, body(): from_pal = lax.ppermute(to_pal, RING, even_edges())  6.96 us
    ppermute x1, waiting for transfers between devices, ask(): lax.ppermute(gather(table, asked, own, count), RING, odd_edges())  5.99 us
    pallas_call x1, Pallas kernels, exchange_terms(): pl.pallas_call(exchange_kernel, in_specs=[pl.BlockSpec(memory_space=pltpu...  4.73 us
  transfers between devices with their start and end apart: 9, of which 6 were waited for; matrix products, arithmetic and copies ran while one was open for 2% of the time, Pallas kernels for 5%

profile of v3, /device:TPU:71, one launch (start us, length us, event | category | flops | bytes accessed | tf_op | source)
XLA Modules:
  0.0 107.8 jit_solution(7659641681009596752)
XLA Ops:
  0.0 0.0 copy-start
  0.0 1.6 %copy-done = f32[8,8,64,64]{3,2,1,0:T(8,128)S(1)} copy-done((f32[8,8,64,64]{3,2,1,0:T(8,128)S(1)}, f32[8,8,64,64]{3,2,1,0:T(8,128)}, u32[]{:S(2)}) %copy-start) | copy-done | bytes 1048600
  1.6 0.0 copy-start.2
  1.6 0.0 copy-start.3
  1.6 0.0 copy-start.1
  1.6 0.4 shard_map.46
  2.0 2.6 %collective-permute-start.29 = (f32[8,4,64,128]{3,2,1,0:T(8,128)S(1)}, f32[8,4,64,128]{3,2,1,0:T(8,128)S(1)}, u32[]{:S(2)}, u32[]{:S(2)}) collective-permute-start(f32[8,4,64,128]{3,2,1,0:T(8,128)S(1)} %shard_map.46), channel_id=1, source_target_pairs={{0,8},{8,0},{16,24},{24,16},{32,40},{40,32},{48,56},{56,48},{64,72... | collective-permute-start | bytes 3145736 | tf_op jit(solution)/shard_map/ppermute | solution.py:457
  4.6 0.0 copy-done.2
  4.7 0.0 copy-done.3
  4.7 0.7 fusion.1
  5.3 3.1 %collective-permute-start.28 = (s32[8]{0:T(128)S(1)}, s32[8]{0:T(128)S(1)}, u32[]{:S(2)}, u32[]{:S(2)}) collective-permute-start(s32[8]{0:T(128)S(1)} %get-tuple-element.169), channel_id=1, source_target_pairs={{0,504},{8,16},{16,8},{24,32},{32,24},{40,48},{48,40},{56,64},{64,... | collective-permute-start | bytes 104 | tf_op jit(solution)/shard_map/ppermute | solution.py:455
  9.0 0.1 pad_add_fusion
  9.1 0.1 pad.3.clone
  9.2 0.1 convert_subtract_fusion
  9.2 0.0 copy-done.1
  9.2 0.1 multiply_reduce_fusion
  9.4 0.1 add_add_fusion.table_ref
  9.5 0.7 collective-permute-done.28.asked_ref
  10.2 0.6 fusion
  12.1 11.1 %conditional.3 = (f32[7,4,64,128]{3,2,1,0:T(8,128)}) conditional(s32[]{:T(128)} %clamp.8, (s32[6,8]{1,0:T(8,128)S(1)}, s32[8]{0:T(128)S(1)}, f32[8,4,64,128]{3,2,1,0:T(8,128)S(1)}) %tuple.73, (s32[6,8]{1,0:T(8,128)S(1)}, s32[8]{0:T(128)S(1)}, f32[8,4,64,128]{3,2,1,0:T(8,128)S(1)}) %tuple.73, (s32[6,8]{1,0:T(8,128)S(1)}, ...), branch_computations={%region_4.5_spmd, %region_5.6_spmd, %region_6.7_spmd, %region_7.8_... | conditional | bytes 3670064 | solution.py:467
  12.1 1.2 %branch_2_fun.7 = f32[3,4,64,128]{3,2,1,0:T(8,128)S(1)} custom-call(s32[6,8]{1,0:T(8,128)S(1)} %get-tuple-element.125.table_ref, s32[8]{0:T(128)S(1)} %get-tuple-element.126.asked_ref, f32[8,4,64,128]{3,2,1,0:T(8,128)S(1)} %get-tuple-element.127.own_ref), custom_call_target="tpu_custom_call" | custom-call | tf_op jit(solution)/shard_map/cond/branch_2_fun/pallas_call | solution.py:121
  13.3 3.1 %collective-permute-start.2 = (f32[3,4,64,128]{3,2,1,0:T(8,128)S(1)}, f32[3,4,64,128]{3,2,1,0:T(8,128)S(1)}, u32[]{:S(2)}, u32[]{:S(2)}) collective-permute-start(f32[3,4,64,128]{3,2,1,0:T(8,128)S(1)} %branch_2_fun.7), channel_id=1, source_target_pairs={{0,504},{8,16},{16,8},{24,32},{32,24},{40,48},{48,40},{56,64},{64,... | collective-permute-start | bytes 1179656 | tf_op jit(solution)/shard_map/cond/branch_2_fun/ppermute | solution.py:152
  16.4 6.0 %collective-permute-done.2.in_ref = f32[3,4,64,128]{3,2,1,0:T(8,128)S(1)} collective-permute-done((f32[3,4,64,128]{3,2,1,0:T(8,128)S(1)}, f32[3,4,64,128]{3,2,1,0:T(8,128)S(1)}, u32[]{:S(2)}, u32[]{:S(2)}) %collective-permute-start.2) | collective-permute-done | bytes 393248 | tf_op jit(solution)/shard_map/cond/branch_2_fun/ppermute | solution.py:152
  22.4 0.8 branch_2_fun.8
  23.2 0.0 collective-permute-done.29
  23.2 64.3 %conditional.4 = ((f32[8,4,64,128]{3,2,1,0:T(8,128)}, f32[8,4,64,128]{3,2,1,0:T(8,128)}, f32[7,4,64,128]{3,2,1,0:T(8,128)S(1)})) conditional(s32[]{:T(128)} %clamp.7, (s32[6,8]{1,0:T(8,128)S(1)}, f32[8,4,64,128]{3,2,1,0:T(8,128)S(1)}, f32[8,4,64,128]{3,2,1,0:T(8,128)S(1)}, f32[7,4,64,128]{3,2,1,0:T(8,128)}) %tuple.74, ...), branch_computations={%region_11.12_spmd, %region_12.13_spmd, %region_13.14_spmd, %regio... | conditional | bytes 8388776 | solution.py:472
  23.2 2.8 %branch_2_fun.9 = (f32[2,8,64,128]{3,2,1,0:T(8,128)S(1)}, f32[1,8,64,128]{3,2,1,0:T(8,128)S(1)}) custom-call(s32[6,8]{1,0:T(8,128)S(1)} %get-tuple-element.150.table_ref, f32[8,4,64,128]{3,2,1,0:T(8,128)S(1)} %get-tuple-element.151.own_ref, f32[8,4,64,128]{3,2,1,0:T(8,128)S(1)} %get-tuple-element.152.pal_ref, f32[7,4,64,128]{3,2,1,0:T(8,128)} %get-tuple-element.153.far_ref), custom_call_target="tpu_custom_call" | custom-call | tf_op jit(solution)/shard_map/cond/branch_2_fun/pallas_call | solution.py:238
  26.1 7.5 %collective-permute-start.13 = (f32[2,8,64,128]{3,2,1,0:T(8,128)S(1)}, f32[2,8,64,128]{3,2,1,0:T(8,128)S(1)}, u32[]{:S(2)}, u32[]{:S(2)}) collective-permute-start(f32[2,8,64,128]{3,2,1,0:T(8,128)S(1)} %get-tuple-element.154.own_ref), channel_id=1, source_target_pairs={{0,1},{1,0},{2,3},{3,2},{4,5},{5,4},{6,7},{7,6},{8,9},{9,8},{10,11... | collective-permute-start | bytes 1572872 | tf_op jit(solution)/shard_map/cond/branch_2_fun/ppermute | solution.py:446
  33.5 1.9 %collective-permute-start.15 = (f32[1,8,64,128]{3,2,1,0:T(8,128)S(1)}, f32[1,8,64,128]{3,2,1,0:T(8,128)S(1)}, u32[]{:S(2)}, u32[]{:S(2)}) collective-permute-start(f32[1,8,64,128]{3,2,1,0:T(8,128)S(1)} %get-tuple-element.155.own_ref), channel_id=1, source_target_pairs={{0,1},{1,0},{2,3},{3,2},{4,5},{5,4},{6,7},{7,6},{8,9},{9,8},{10,11... | collective-permute-start | bytes 786440 | tf_op jit(solution)/shard_map/cond/branch_2_fun/ppermute | solution.py:446
  35.4 22.9 %collective-permute-done.13.near_ref = f32[2,8,64,128]{3,2,1,0:T(8,128)S(1)} collective-permute-done((f32[2,8,64,128]{3,2,1,0:T(8,128)S(1)}, f32[2,8,64,128]{3,2,1,0:T(8,128)S(1)}, u32[]{:S(2)}, u32[]{:S(2)}) %collective-permute-start.13) | collective-permute-done | bytes 524320 | tf_op jit(solution)/shard_map/cond/branch_2_fun/ppermute | solution.py:446
  58.3 1.3 %collective-permute-start.14 = (f32[2,8,64,128]{3,2,1,0:T(8,128)S(1)}, f32[2,8,64,128]{3,2,1,0:T(8,128)S(1)}, u32[]{:S(2)}, u32[]{:S(2)}) collective-permute-start(f32[2,8,64,128]{3,2,1,0:T(8,128)S(1)} %collective-permute-done.13.near_ref), channel_id=1, source_target_pairs={{0,2},{2,4},{3,1},{4,6},{5,3},{7,5},{8,10},{10,12},{11,9},{12,14},... | collective-permute-start | bytes 1572872 | tf_op jit(solution)/shard_map/cond/branch_2_fun/ppermute | solution.py:447
  59.6 4.3 %collective-permute-done.15.near_ref = f32[1,8,64,128]{3,2,1,0:T(8,128)S(1)} collective-permute-done((f32[1,8,64,128]{3,2,1,0:T(8,128)S(1)}, f32[1,8,64,128]{3,2,1,0:T(8,128)S(1)}, u32[]{:S(2)}, u32[]{:S(2)}) %collective-permute-start.15) | collective-permute-done | bytes 262176 | tf_op jit(solution)/shard_map/cond/branch_2_fun/ppermute | solution.py:446
  64.0 1.5 %collective-permute-start.16 = (f32[1,8,64,128]{3,2,1,0:T(8,128)S(1)}, f32[1,8,64,128]{3,2,1,0:T(8,128)S(1)}, u32[]{:S(2)}, u32[]{:S(2)}) collective-permute-start(f32[1,8,64,128]{3,2,1,0:T(8,128)S(1)} %collective-permute-done.15.near_ref), channel_id=1, source_target_pairs={{0,2},{2,4},{3,1},{4,6},{5,3},{7,5},{8,10},{10,12},{11,9},{12,14},... | collective-permute-start | bytes 786440 | tf_op jit(solution)/shard_map/cond/branch_2_fun/ppermute | solution.py:447
  65.4 9.7 %collective-permute-done.16.far_ref = f32[1,8,64,128]{3,2,1,0:T(8,128)S(1)} collective-permute-done((f32[1,8,64,128]{3,2,1,0:T(8,128)S(1)}, f32[1,8,64,128]{3,2,1,0:T(8,128)S(1)}, u32[]{:S(2)}, u32[]{:S(2)}) %collective-permute-start.16) | collective-permute-done | bytes 262176 | tf_op jit(solution)/shard_map/cond/branch_2_fun/ppermute | solution.py:447
  75.1 2.6 %branch_2_fun.11.rest_1_ = f32[1,8,64,128]{3,2,1,0:T(8,128)S(1)} custom-call(s32[6,8]{1,0:T(8,128)S(1)} %get-tuple-element.150.table_ref, f32[1,8,64,128]{3,2,1,0:T(8,128)S(1)} %collective-permute-done.16.far_ref, f32[1,8,64,128]{3,2,1,0:T(8,128)S(1)} %get-tuple-element.155.own_ref, f32[1,8,64,128]{3,2,1,0:T(8,128)S(1)} %collective-permute-done.15.near_ref), custom_call_target="tpu_custom_call" | custom-call | tf_op jit(solution)/shard_map/cond/branch_2_fun/pallas_call | solution.py:405
  77.7 0.0 collective-permute-done.14.far_ref
  77.7 4.6 %branch_2_fun.10.rest_0_ = f32[2,8,64,128]{3,2,1,0:T(8,128)S(1)} custom-call(s32[6,8]{1,0:T(8,128)S(1)} %get-tuple-element.150.table_ref, f32[2,8,64,128]{3,2,1,0:T(8,128)S(1)} %collective-permute-done.14.far_ref, f32[2,8,64,128]{3,2,1,0:T(8,128)S(1)} %get-tuple-element.154.own_ref, f32[2,8,64,128]{3,2,1,0:T(8,128)S(1)} %collective-permute-done.13.near_ref), custom_call_target="tpu_custom_call" | custom-call | tf_op jit(solution)/shard_map/cond/branch_2_fun/pallas_call | solution.py:405
  82.3 4.7 %branch_2_fun.12 = (f32[8,4,64,128]{3,2,1,0:T(8,128)}, f32[8,4,64,128]{3,2,1,0:T(8,128)}, f32[7,4,64,128]{3,2,1,0:T(8,128)S(1)}) custom-call(s32[6,8]{1,0:T(8,128)S(1)} %get-tuple-element.150.table_ref, f32[8,4,64,128]{3,2,1,0:T(8,128)S(1)} %get-tuple-element.151.own_ref, f32[8,4,64,128]{3,2,1,0:T(8,128)S(1)} %get-tuple-element.152.pal_ref, ...), custom_call_target="tpu_custom_call" | custom-call | tf_op jit(solution)/shard_map/cond/branch_2_fun/pallas_call | solution.py:314
  87.5 7.0 %collective-permute-start.30 = (f32[8,4,64,128]{3,2,1,0:T(8,128)}, f32[8,4,64,128]{3,2,1,0:T(8,128)S(1)}, u32[]{:S(2)}, u32[]{:S(2)}) collective-permute-start(f32[8,4,64,128]{3,2,1,0:T(8,128)} %get-tuple-element.166), channel_id=1, source_target_pairs={{0,8},{8,0},{16,24},{24,16},{32,40},{40,32},{48,56},{56,48},{64,72... | collective-permute-start | bytes 3145736 | tf_op jit(solution)/shard_map/ppermute | solution.py:474
  94.5 9.9 %conditional.5 = (f32[7,4,64,128]{3,2,1,0:T(8,128)}) conditional(s32[]{:T(128)} %clamp.8, f32[7,4,64,128]{3,2,1,0:T(8,128)S(1)} %get-tuple-element.167, f32[7,4,64,128]{3,2,1,0:T(8,128)S(1)} %get-tuple-element.167, f32[7,4,64,128]{3,2,1,0:T(8,128)S(1)} %get-tuple-element.167, ...), branch_computations={%region_15.16_spmd, %region_16.17_spmd, %region_17.18_spmd, %regio... | conditional | bytes 4718640 | solution.py:476
  94.6 1.9 %collective-permute-start.23 = (f32[3,4,64,128]{3,2,1,0:T(8,128)S(1)}, f32[3,4,64,128]{3,2,1,0:T(8,128)S(1)}, u32[]{:S(2)}, u32[]{:S(2)}) collective-permute-start(f32[3,4,64,128]{3,2,1,0:T(8,128)S(1)} %slice.21), channel_id=1, source_target_pairs={{0,504},{8,16},{16,8},{24,32},{32,24},{40,48},{48,40},{56,64},{64,... | collective-permute-start | bytes 1179656 | tf_op jit(solution)/shard_map/cond/branch_2_fun/ppermute | solution.py:156
  96.5 7.2 %collective-permute-done.23.in_ref = f32[3,4,64,128]{3,2,1,0:T(8,128)S(1)} collective-permute-done((f32[3,4,64,128]{3,2,1,0:T(8,128)S(1)}, f32[3,4,64,128]{3,2,1,0:T(8,128)S(1)}, u32[]{:S(2)}, u32[]{:S(2)}) %collective-permute-start.23) | collective-permute-done | bytes 393248 | tf_op jit(solution)/shard_map/cond/branch_2_fun/ppermute | solution.py:156
  103.7 0.8 branch_2_fun.13
  104.5 0.0 collective-permute-done.30.pal_ref
  104.5 3.4 %shard_map.47 = f32[8,8,64,64]{3,2,1,0:T(8,128)} custom-call(s32[6,8]{1,0:T(8,128)S(1)} %add_add_fusion.table_ref, s32[8]{0:T(128)S(1)} %collective-permute-done.28.asked_ref, f32[8,4,64,128]{3,2,1,0:T(8,128)} %get-tuple-element.165.mid_ref, f32[8,4,64,128]{3,2,1,0:T(8,128)S(1)} %collective-permute-done.30.pal_ref, f32[7,4,64,128]{3,2,1,0:T(8,128)} %get-tuple-element.188.far_ref), custom_call_target="tpu_custom_call" | custom-call | tf_op jit(solution)/shard_map/pallas_call | solution.py:89
  (2 shorter events, 0.0 us)
Async XLA Ops:
  0.0 1.6 %copy-start = (f32[8,8,64,64]{3,2,1,0:T(8,128)S(1)}, f32[8,8,64,64]{3,2,1,0:T(8,128)}, u32[]{:S(2)}) copy-start(f32[8,8,64,64]{3,2,1,0:T(8,128)} %field_ref.1) | copy-start | bytes 3145732
  1.6 3.1 %copy-start.2 = (s32[8,2]{0,1:T(2,128)S(1)}, s32[8,2]{0,1:T(2,128)}, u32[]{:S(2)}) copy-start(s32[8,2]{0,1:T(2,128)} %param.24) | copy-start | bytes 196
  1.6 3.1 %copy-start.3 = (s32[8]{0:T(128)S(1)}, s32[8]{0:T(128)}, u32[]{:S(2)}) copy-start(s32[8]{0:T(128)} %param.25) | copy-start | bytes 100
  1.6 7.6 %copy-start.1 = (s32[512,2]{0,1:T(2,128)S(1)}, s32[512,2]{0,1:T(2,128)}, u32[]{:S(2)}) copy-start(s32[512,2]{0,1:T(2,128)} %param.23) | copy-start | bytes 12292
  2.0 21.2 %collective-permute-start.29 = (f32[8,4,64,128]{3,2,1,0:T(8,128)S(1)}, f32[8,4,64,128]{3,2,1,0:T(8,128)S(1)}, u32[]{:S(2)}, u32[]{:S(2)}) collective-permute-start(f32[8,4,64,128]{3,2,1,0:T(8,128)S(1)} %shard_map.46), channel_id=1, source_target_pairs={{0,8},{8,0},{16,24},{24,16},{32,40},{40,32},{48,56},{56,48},{64,72... | collective-permute-start | bytes 3145736 | tf_op jit(solution)/shard_map/ppermute | solution.py:457
  5.3 4.8 %collective-permute-start.28 = (s32[8]{0:T(128)S(1)}, s32[8]{0:T(128)S(1)}, u32[]{:S(2)}, u32[]{:S(2)}) collective-permute-start(s32[8]{0:T(128)S(1)} %get-tuple-element.169), channel_id=1, source_target_pairs={{0,504},{8,16},{16,8},{24,32},{32,24},{40,48},{48,40},{56,64},{64,... | collective-permute-start | bytes 104 | tf_op jit(solution)/shard_map/ppermute | solution.py:455
  13.3 9.1 %collective-permute-start.2 = (f32[3,4,64,128]{3,2,1,0:T(8,128)S(1)}, f32[3,4,64,128]{3,2,1,0:T(8,128)S(1)}, u32[]{:S(2)}, u32[]{:S(2)}) collective-permute-start(f32[3,4,64,128]{3,2,1,0:T(8,128)S(1)} %branch_2_fun.7), channel_id=1, source_target_pairs={{0,504},{8,16},{16,8},{24,32},{32,24},{40,48},{48,40},{56,64},{64,... | collective-permute-start | bytes 1179656 | tf_op jit(solution)/shard_map/cond/branch_2_fun/ppermute | solution.py:152
  26.1 32.3 %collective-permute-start.13 = (f32[2,8,64,128]{3,2,1,0:T(8,128)S(1)}, f32[2,8,64,128]{3,2,1,0:T(8,128)S(1)}, u32[]{:S(2)}, u32[]{:S(2)}) collective-permute-start(f32[2,8,64,128]{3,2,1,0:T(8,128)S(1)} %get-tuple-element.154.own_ref), channel_id=1, source_target_pairs={{0,1},{1,0},{2,3},{3,2},{4,5},{5,4},{6,7},{7,6},{8,9},{9,8},{10,11... | collective-permute-start | bytes 1572872 | tf_op jit(solution)/shard_map/cond/branch_2_fun/ppermute | solution.py:446
  33.5 30.4 %collective-permute-start.15 = (f32[1,8,64,128]{3,2,1,0:T(8,128)S(1)}, f32[1,8,64,128]{3,2,1,0:T(8,128)S(1)}, u32[]{:S(2)}, u32[]{:S(2)}) collective-permute-start(f32[1,8,64,128]{3,2,1,0:T(8,128)S(1)} %get-tuple-element.155.own_ref), channel_id=1, source_target_pairs={{0,1},{1,0},{2,3},{3,2},{4,5},{5,4},{6,7},{7,6},{8,9},{9,8},{10,11... | collective-permute-start | bytes 786440 | tf_op jit(solution)/shard_map/cond/branch_2_fun/ppermute | solution.py:446
  58.3 19.4 %collective-permute-start.14 = (f32[2,8,64,128]{3,2,1,0:T(8,128)S(1)}, f32[2,8,64,128]{3,2,1,0:T(8,128)S(1)}, u32[]{:S(2)}, u32[]{:S(2)}) collective-permute-start(f32[2,8,64,128]{3,2,1,0:T(8,128)S(1)} %collective-permute-done.13.near_ref), channel_id=1, source_target_pairs={{0,2},{2,4},{3,1},{4,6},{5,3},{7,5},{8,10},{10,12},{11,9},{12,14},... | collective-permute-start | bytes 1572872 | tf_op jit(solution)/shard_map/cond/branch_2_fun/ppermute | solution.py:447
  64.0 11.2 %collective-permute-start.16 = (f32[1,8,64,128]{3,2,1,0:T(8,128)S(1)}, f32[1,8,64,128]{3,2,1,0:T(8,128)S(1)}, u32[]{:S(2)}, u32[]{:S(2)}) collective-permute-start(f32[1,8,64,128]{3,2,1,0:T(8,128)S(1)} %collective-permute-done.15.near_ref), channel_id=1, source_target_pairs={{0,2},{2,4},{3,1},{4,6},{5,3},{7,5},{8,10},{10,12},{11,9},{12,14},... | collective-permute-start | bytes 786440 | tf_op jit(solution)/shard_map/cond/branch_2_fun/ppermute | solution.py:447
  87.5 16.9 %collective-permute-start.30 = (f32[8,4,64,128]{3,2,1,0:T(8,128)}, f32[8,4,64,128]{3,2,1,0:T(8,128)S(1)}, u32[]{:S(2)}, u32[]{:S(2)}) collective-permute-start(f32[8,4,64,128]{3,2,1,0:T(8,128)} %get-tuple-element.166), channel_id=1, source_target_pairs={{0,8},{8,0},{16,24},{24,16},{32,40},{40,32},{48,56},{56,48},{64,72... | collective-permute-start | bytes 3145736 | tf_op jit(solution)/shard_map/ppermute | solution.py:474
  94.6 9.1 %collective-permute-start.23 = (f32[3,4,64,128]{3,2,1,0:T(8,128)S(1)}, f32[3,4,64,128]{3,2,1,0:T(8,128)S(1)}, u32[]{:S(2)}, u32[]{:S(2)}) collective-permute-start(f32[3,4,64,128]{3,2,1,0:T(8,128)S(1)} %slice.21), channel_id=1, source_target_pairs={{0,504},{8,16},{16,8},{24,32},{32,24},{40,48},{48,40},{56,64},{64,... | collective-permute-start | bytes 1179656 | tf_op jit(solution)/shard_map/cond/branch_2_fun/ppermute | solution.py:156

commit v4 on v3

--- a/solution.py
+++ b/solution.py
@@ -64,34 +64,37 @@
 
 
 def finish_kernel(table_ref, asked_ref, mid_ref, pal_ref, far_ref, out_ref, acc):
-    orbs, half = mid_ref.shape[:2]
+    step, half = mid_ref.shape[:2]
+    start = pl.program_id(0) * step
+    orbs = pl.num_programs(0) * step
     acc[...] = mid_ref[...] + pal_ref[...]
     rank = 0
     for slot in range(asked_ref.shape[0]):
         local = asked_ref[slot] - orbs * table_ref[GROUP, 0]
-        hit = (local >= 0) & (local < orbs)
         if slot:
             rank = jnp.minimum(rank, far_ref.shape[0] - 1)
 
-        @pl.when(hit)
+        @pl.when((local >= start) & (local < start + step))
         def _():
-            acc[local] += far_ref[rank]
-
-        rank += hit.astype(jnp.int32)
+            acc[local - start] += far_ref[rank]
+
+        rank += ((local >= 0) & (local < orbs)).astype(jnp.int32)
     out_ref[:, :half] = acc[..., :BOX]
     out_ref[:, half:] = acc[..., BOX:]
 
 
 def finish(table, asked, middle, from_pal, from_far):
     orbs, half = middle.shape[:2]
+    step = 2
     smem = pl.BlockSpec(memory_space=pltpu.SMEM)
-    vmem = pl.BlockSpec(memory_space=pltpu.VMEM)
+    spec = pl.BlockSpec((step, half, BOX, LANES), lambda i: (i, 0, 0, 0))
     return pl.pallas_call(
         finish_kernel,
-        in_specs=[smem, smem, vmem, vmem, vmem],
-        out_specs=vmem,
+        grid=(orbs // step,),
+        in_specs=[smem, smem, spec, spec, pl.BlockSpec(memory_space=pltpu.VMEM)],
+        out_specs=pl.BlockSpec((step, 2 * half, BOX, BOX), lambda i: (i, 0, 0, 0)),
         out_shape=jax.ShapeDtypeStruct((orbs, 2 * half, BOX, BOX), jnp.float32),
-        scratch_shapes=[pltpu.VMEM(middle.shape, jnp.float32)],
+        scratch_shapes=[pltpu.VMEM((step, half, BOX, LANES), jnp.float32)],
         compiler_params=params(),
     )(table, asked, middle, from_pal, from_far)
 
@@ -157,65 +160,52 @@
 
 
 FIRST, SECOND, BY_Y, BY_Z, GROUP, SLAB = range(6)
+MINE, PAL, FAR = range(3)
 
 
 def locate(table_ref, where_ref, orbs):
     group = table_ref[GROUP, 0]
-    pal = group ^ 1
     rank = 0
-    for slot in range(where_ref.shape[0]):
+    for slot in range(where_ref.shape[1]):
         second = table_ref[SECOND, slot]
         mine = second - orbs * group
-        other = second - orbs * pal
+        other = second - orbs * (group ^ 1)
         is_mine = (mine >= 0) & (mine < orbs)
         is_pal = (other >= 0) & (other < orbs)
         is_far = (second >= 0) & ~is_mine & ~is_pal
-        place = jnp.where(is_pal, orbs + other, jnp.where(is_far, 2 * orbs + rank, 0))
-        where_ref[slot] = jnp.where(is_mine, mine, place)
+        where_ref[0, slot] = jnp.where(is_pal, PAL, jnp.where(is_far, FAR, MINE))
+        place = jnp.where(is_pal, other, jnp.where(is_far, rank, 0))
+        where_ref[1, slot] = jnp.where(is_mine, mine, place)
         rank += is_far.astype(jnp.int32)
 
 
-def clear_pads(ext):
-    zeros = jnp.zeros((ext.shape[1], PAD, LANES), jnp.float32)
-
-    @pl.loop(0, ext.shape[0])
-    def _(orb):
-        ext[orb, :, :PAD] = zeros
-        ext[orb, :, PAD + BOX :] = zeros
-
-
-def fetch(refs, ext, sems):
-    copies = []
-    done = 0
-    for k, ref in enumerate(refs):
-        orbs = ref.shape[0]
-        target = ext.at[pl.ds(done, orbs), :, pl.ds(PAD, BOX), :]
-        copies.append(pltpu.make_async_copy(ref, target, sems.at[k]))
-        done += orbs
-    for copy in copies:
-        copy.start()
-    return copies
+def clear_edges(padded):
+    for x in range(padded.shape[0]):
+        padded[x, :PAD] = jnp.zeros((PAD, LANES), jnp.float32)
+        padded[x, PAD + BOX :] = jnp.zeros((PAD, LANES), jnp.float32)
 
 
 def swapped(field):
     return pltpu.roll(field, LANES // 2, 1)
 
 
-def density_kernel(table_ref, own_ref, pal_ref, far_ref, *rest):
-    out_refs, (ext, where, sems) = rest[:-3], rest[-3:]
-    copies = fetch((own_ref, pal_ref, far_ref), ext, sems)
-    clear_pads(ext)
+def density_kernel(table_ref, own_ref, pal_ref, far_ref, partner_ref, *rest):
+    out_refs, (padded, where) = rest[:-2], rest[-2:]
+    planes = own_ref.shape[1]
     locate(table_ref, where, own_ref.shape[0])
-    for copy in copies:
-        copy.wait()
-    planes = own_ref.shape[1]
+    clear_edges(padded)
     low = lane_index((BOX, LANES)) < BOX
 
-    def density(slot, x):
-        first = table_ref[FIRST, slot]
-        second = where[slot]
-        partner = ext[second, x, pl.ds(PAD - table_ref[BY_Y, slot], BOX), :]
-        return ext[first, x, PAD : PAD + BOX, :] * moved_z(partner, table_ref[BY_Z, slot])
+    def place_partner(slot):
+        for kind, ref in ((MINE, own_ref), (PAL, pal_ref), (FAR, far_ref)):
+
+            @pl.when(where[0, slot] == kind)
+            def _():
+                padded[:, PAD : PAD + BOX] = ref[where[1, slot]]
+
+        rows = pl.ds(PAD - table_ref[BY_Y, slot], BOX)
+        for x in range(planes):
+            partner_ref[slot, x] = moved_z(padded[x, rows, :], table_ref[BY_Z, slot])
 
     done = 0
     for out_ref in out_refs:
@@ -224,9 +214,11 @@
         @pl.loop(0, count)
         def _(pair):
             slot = 2 * (done + pair)
+            place_partner(slot)
+            place_partner(slot + 1)
             for x in range(planes):
-                one = density(slot, x)
-                two = density(slot + 1, x)
+                one = own_ref[table_ref[FIRST, slot], x] * partner_ref[slot, x]
+                two = own_ref[table_ref[FIRST, slot + 1], x] * partner_ref[slot + 1, x]
                 out_ref[pair, x] = jnp.where(low, one, swapped(two))
                 out_ref[pair, planes + x] = jnp.where(low, swapped(one), two)
 
@@ -234,56 +226,60 @@
 
 
 def densities(table, own, pal, far, chunks):
-    orbs, planes = own.shape[:2]
+    planes = own.shape[1]
+    vmem = pl.BlockSpec(memory_space=pltpu.VMEM)
+    shapes = [(2 * sum(chunks), planes, BOX, LANES)]
+    shapes += [(count, 2 * planes, BOX, LANES) for count in chunks]
     return pl.pallas_call(
         density_kernel,
-        in_specs=[pl.BlockSpec(memory_space=pltpu.SMEM)] + [pl.BlockSpec(memory_space=pl.ANY)] * 3,
-        out_specs=[pl.BlockSpec(memory_space=pltpu.VMEM)] * len(chunks),
-        out_shape=[
-            jax.ShapeDtypeStruct((count, 2 * planes, BOX, LANES), jnp.float32) for count in chunks
+        in_specs=[pl.BlockSpec(memory_space=pltpu.SMEM)] + [vmem] * 3,
+        out_specs=[vmem] * len(shapes),
+        out_shape=[jax.ShapeDtypeStruct(shape, jnp.float32) for shape in shapes],
+        scratch_shapes=[
+            pltpu.VMEM((planes, ROWS, LANES), jnp.float32),
+            pltpu.SMEM((2, table.shape[1]), jnp.int32),
         ],
-        scratch_shapes=[
-            pltpu.VMEM((2 * orbs + far.shape[0], planes, ROWS, LANES), jnp.float32),
-            pltpu.SMEM((table.shape[1],), jnp.int32),
-            pltpu.SemaphoreType.DMA((3,)),
-        ],
         compiler_params=params(),
     )(table, own, pal, far)
 
 
-def exchange_kernel(table_ref, own_ref, pal_ref, far_ref, *rest):
-    pot_refs = rest[:-8]
-    mid_ref, to_pal_ref, to_far_ref, ext, acc, moved, where, sems = rest[-8:]
-    copies = fetch((own_ref, pal_ref, far_ref), ext, sems)
-    clear_pads(ext)
-    locate(table_ref, where, own_ref.shape[0])
+def exchange_kernel(table_ref, own_ref, partner_ref, *rest):
+    pot_refs = rest[:-5]
+    mid_ref, to_pal_ref, to_far_ref, padded, where = rest[-5:]
     orbs, planes = mid_ref.shape[:2]
+    locate(table_ref, where, orbs)
+    clear_edges(padded)
     zeros = jnp.zeros((planes, BOX, LANES), jnp.float32)
     low = lane_index((BOX, LANES)) < BOX
 
-    @pl.loop(0, acc.shape[0])
+    @pl.loop(0, orbs)
     def _(orb):
-        acc[orb] = zeros
-
-    for x in range(planes):
-        moved[x, :PAD] = jnp.zeros((PAD, LANES), jnp.float32)
-        moved[x, PAD + BOX :] = jnp.zeros((PAD, LANES), jnp.float32)
-    for copy in copies:
-        copy.wait()
+        mid_ref[orb] = zeros
+        to_pal_ref[orb] = zeros
 
     def add_terms(slot, potential):
         first = table_ref[FIRST, slot]
-        second = where[slot]
         by_y = table_ref[BY_Y, slot]
         by_z = table_ref[BY_Z, slot]
         weight = jnp.where(table_ref[SECOND, slot] >= 0, 1.0, 0.0)
         for x in range(planes):
             pot = weight * potential(x)
-            partner = moved_z(ext[second, x, pl.ds(PAD - by_y, BOX), :], by_z)
-            acc[first, x] += pot * partner
-            moved[x, PAD : PAD + BOX] = moved_z(pot * ext[first, x, PAD : PAD + BOX, :], -by_z)
-        for x in range(planes):
-            acc[second, x] += moved[x, pl.ds(PAD + by_y, BOX), :]
+            mid_ref[first, x] += pot * partner_ref[slot, x]
+            padded[x, PAD : PAD + BOX] = moved_z(pot * own_ref[first, x], -by_z)
+        rows = pl.ds(PAD + by_y, BOX)
+        at = where[1, slot]
+
+        @pl.when(where[0, slot] == MINE)
+        def _():
+            mid_ref[at] += padded[:, rows, :]
+
+        @pl.when(where[0, slot] == PAL)
+        def _():
+            to_pal_ref[at] += padded[:, rows, :]
+
+        @pl.when(where[0, slot] == FAR)
+        def _():
+            to_far_ref[at] = padded[:, rows, :]
 
     done = 0
     for pot_ref in pot_refs:
@@ -303,30 +299,24 @@
 
         done += count
 
-    mid_ref[...] = acc[:orbs]
-    to_pal_ref[...] = acc[orbs : 2 * orbs]
-    to_far_ref[...] = acc[2 * orbs :]
-
-
-def exchange_terms(table, potentials, own, pal, far):
-    orbs, planes = own.shape[:2]
+
+def exchange_terms(table, potentials, own, partner, most):
+    planes = own.shape[1]
     vmem = pl.BlockSpec(memory_space=pltpu.VMEM)
     return pl.pallas_call(
         exchange_kernel,
-        in_specs=[pl.BlockSpec(memory_space=pltpu.SMEM)]
-        + [pl.BlockSpec(memory_space=pl.ANY)] * 3
-        + [vmem] * len(potentials),
+        in_specs=[pl.BlockSpec(memory_space=pltpu.SMEM)] + [vmem] * (2 + len(potentials)),
         out_specs=[vmem] * 3,
-        out_shape=[jax.ShapeDtypeStruct(a.shape, jnp.float32) for a in (own, pal, far)],
+        out_shape=[
+            jax.ShapeDtypeStruct((count,) + own.shape[1:], jnp.float32)
+            for count in (own.shape[0], own.shape[0], most)
+        ],
         scratch_shapes=[
-            pltpu.VMEM((2 * orbs + far.shape[0], planes, ROWS, LANES), jnp.float32),
-            pltpu.VMEM((2 * orbs + far.shape[0], planes, BOX, LANES), jnp.float32),
             pltpu.VMEM((planes, ROWS, LANES), jnp.float32),
-            pltpu.SMEM((table.shape[1],), jnp.int32),
-            pltpu.SemaphoreType.DMA((3,)),
+            pltpu.SMEM((2, table.shape[1]), jnp.int32),
         ],
         compiler_params=params(),
-    )(table, own, pal, far, *potentials)
+    )(table, own, partner, *potentials)
 
 
 SUB = 8
@@ -441,12 +431,11 @@
     across = [(s, s ^ 1) for s in range(slabs)]
     onward = [(s, s + 2 - 4 * (s % 2)) for s in range(slabs)]
     onward = [(s, t) for s, t in onward if 0 <= t < slabs]
-    chunks = [count] if count == 1 else [count - count // 2, count // 2]
-    made = densities(table, own, pal, far, chunks)
+    partner, *made = densities(table, own, pal, far, [1] * count)
     near = [lax.ppermute(dens, "slab", across) for dens in made]
     next_but_one = [lax.ppermute(dens, "slab", onward) for dens in near]
     potentials = [solve(table, f, d, n, slabs) for f, d, n in zip(next_but_one, made, near)]
-    return exchange_terms(table, potentials, own, pal, far)
+    return exchange_terms(table, potentials, own, partner, far.shape[0])
 
 
 def body(orbitals, offsets, pairs, live):
@@ -454,7 +443,8 @@
     seconds = jnp.where(live > 0, pairs[:, 1], -1)
     asked = lax.ppermute(seconds, RING, odd_edges())
     own = pack(orbitals)
-    pal = lax.ppermute(own, RING, even_edges())
+    offered, asked = lax.optimization_barrier((own, asked))
+    pal = lax.ppermute(offered, RING, even_edges())
     table = slot_table(offsets, pairs, seconds, orbs)
 
     group = lax.axis_index(RING)

time: 108 us -> 107 us (level)
  the two profiles are of different devices: /device:TPU:71 before, /device:TPU:64 now
where the time goes in v4:
time: 107 us
  starting transfers between devices  56.8 us (53%)
  waiting for transfers between devices  30.4 us (28%)
  Pallas kernels  13.3 us (12%)
  other arithmetic  2.46 us (2%)
  between operations  2.01 us (2%)
  local copies, waits for them, and re-layouts  1.71 us (2%)
    ppermute x1, starting transfers between devices, answer(): return spread(lax.ppermute(terms[:count], RING, odd_edges()), most)  34.6 us
    ppermute x1, waiting for transfers between devices, ask(): lax.ppermute(gather(table, asked, own, count), RING, odd_edges())  10.1 us
    ppermute x1, waiting for transfers between devices, answer(): return spread(lax.ppermute(terms[:count], RING, odd_edges()), most)  9.66 us
    ppermute x1, starting transfers between devices, solved_terms(): near = [lax.ppermute(dens, 'slab', across) for dens in made]  6.92 us
    ppermute x1, waiting for transfers between devices, solved_terms(): near = [lax.ppermute(dens, 'slab', across) for dens in made]  5.28 us
    ppermute x1, starting transfers between devices, ask(): lax.ppermute(gather(table, asked, own, count), RING, odd_edges())  4.04 us
    ppermute x1, starting transfers between devices, body(): asked = lax.ppermute(seconds, RING, odd_edges())  4.03 us
    ppermute x1, waiting for transfers between devices, solved_terms(): next_but_one = [lax.ppermute(dens, 'slab', onward) for dens in near]  3.86 us
  transfers between devices with their start and end apart: 7, of which 5 were waited for; matrix products, arithmetic and copies ran while one was open for 1% of the time, Pallas kernels for 3%

profile of v4, /device:TPU:64, one launch (start us, length us, event | category | flops | bytes accessed | tf_op | source)
XLA Modules:
  0.0 106.8 jit_solution(1330397969028618744)
XLA Ops:
  0.0 0.0 copy-start.2
  0.0 0.0 copy-start.1
  0.0 1.4 %fusion.1 = (s32[]{:T(128)}, s32[8]{0:T(128)S(1)}, s32[]{:T(128)}) fusion(s32[]{:T(128)S(6)} %mul.33, s32[8,2]{0,1:T(2,128)} %param.24, s32[8]{0:T(128)} %param.25), kind=kLoop, calls=%fused_computation.9 | loop fusion | flops 70 | bytes 108 | tf_op jit(solution)/shard_map/reduce_sum | solution.py:426
  1.4 4.0 %collective-permute-start.34 = (s32[8]{0:T(128)S(1)}, s32[8]{0:T(128)S(1)}, u32[]{:S(2)}, u32[]{:S(2)}) collective-permute-start(s32[8]{0:T(128)S(1)} %get-tuple-element.181), channel_id=1, source_target_pairs={{0,504},{8,16},{16,8},{24,32},{32,24},{40,48},{48,40},{56,64},{64,... | collective-permute-start | bytes 104 | tf_op jit(solution)/shard_map/ppermute | solution.py:444
  5.5 0.0 copy-start
  5.5 1.6 %copy-done = f32[8,8,64,64]{3,2,1,0:T(8,128)S(1)} copy-done((f32[8,8,64,64]{3,2,1,0:T(8,128)S(1)}, f32[8,8,64,64]{3,2,1,0:T(8,128)}, u32[]{:S(2)}) %copy-start) | copy-done | bytes 1048600
  7.1 0.4 shard_map.46
  7.5 1.5 %collective-permute-done.34.asked_ref = s32[8]{0:T(128)S(1)} collective-permute-done((s32[8]{0:T(128)S(1)}, s32[8]{0:T(128)S(1)}, u32[]{:S(2)}, u32[]{:S(2)}) %collective-permute-start.34) | collective-permute-done | bytes 64 | tf_op jit(solution)/shard_map/ppermute | solution.py:444
  9.0 1.9 %collective-permute-start.35 = (f32[8,4,64,128]{3,2,1,0:T(8,128)S(1)}, f32[8,4,64,128]{3,2,1,0:T(8,128)S(1)}, u32[]{:S(2)}, u32[]{:S(2)}) collective-permute-start(f32[8,4,64,128]{3,2,1,0:T(8,128)S(1)} %shard_map.46), channel_id=1, source_target_pairs={{0,8},{8,0},{16,24},{24,16},{32,40},{40,32},{48,56},{56,48},{64,72... | collective-permute-start | bytes 3145736 | tf_op jit(solution)/shard_map/ppermute | solution.py:447
  11.6 0.1 pad_add_fusion
  11.6 0.1 pad.3.clone
  11.7 0.0 copy-done.2
  11.7 0.1 convert_subtract_fusion
  11.8 0.0 copy-done.1
  11.8 0.1 multiply_reduce_fusion
  11.9 0.1 add_add_fusion.table_ref
  12.0 0.6 fusion
  13.9 16.3 %conditional.3 = (f32[7,4,64,128]{3,2,1,0:T(8,128)}) conditional(s32[]{:T(128)} %clamp.8, (s32[6,8]{1,0:T(8,128)S(1)}, s32[8]{0:T(128)S(1)}, f32[8,4,64,128]{3,2,1,0:T(8,128)S(1)}) %tuple.75, (s32[6,8]{1,0:T(8,128)S(1)}, s32[8]{0:T(128)S(1)}, f32[8,4,64,128]{3,2,1,0:T(8,128)S(1)}) %tuple.75, (s32[6,8]{1,0:T(8,128)S(1)}, ...), branch_computations={%region_4.5_spmd, %region_5.6_spmd, %region_6.7_spmd, %region_7.8_... | conditional | bytes 3670064 | solution.py:457
  14.0 1.4 %branch_3_fun.9 = f32[4,4,64,128]{3,2,1,0:T(8,128)S(1)} custom-call(s32[6,8]{1,0:T(8,128)S(1)} %get-tuple-element.128.table_ref, s32[8]{0:T(128)S(1)} %get-tuple-element.129.asked_ref, f32[8,4,64,128]{3,2,1,0:T(8,128)S(1)} %get-tuple-element.130.own_ref), custom_call_target="tpu_custom_call" | custom-call | tf_op jit(solution)/shard_map/cond/branch_3_fun/pallas_call | solution.py:124
  15.3 4.0 %collective-permute-start.3 = (f32[4,4,64,128]{3,2,1,0:T(8,128)S(1)}, f32[4,4,64,128]{3,2,1,0:T(8,128)S(1)}, u32[]{:S(2)}, u32[]{:S(2)}) collective-permute-start(f32[4,4,64,128]{3,2,1,0:T(8,128)S(1)} %branch_3_fun.9), channel_id=1, source_target_pairs={{0,504},{8,16},{16,8},{24,32},{32,24},{40,48},{48,40},{56,64},{64,... | collective-permute-start | bytes 1572872 | tf_op jit(solution)/shard_map/cond/branch_3_fun/ppermute | solution.py:155
  19.4 10.1 %collective-permute-done.3.in_ref = f32[4,4,64,128]{3,2,1,0:T(8,128)S(1)} collective-permute-done((f32[4,4,64,128]{3,2,1,0:T(8,128)S(1)}, f32[4,4,64,128]{3,2,1,0:T(8,128)S(1)}, u32[]{:S(2)}, u32[]{:S(2)}) %collective-permute-start.3) | collective-permute-done | bytes 524320 | tf_op jit(solution)/shard_map/cond/branch_3_fun/ppermute | solution.py:155
  29.4 0.8 branch_3_fun.10
  30.3 0.0 collective-permute-done.35
  30.3 25.8 %conditional.4 = ((f32[8,4,64,128]{3,2,1,0:T(8,128)S(1)}, f32[8,4,64,128]{3,2,1,0:T(8,128)}, f32[7,4,64,128]{3,2,1,0:T(8,128)S(1)})) conditional(s32[]{:T(128)} %clamp.7, (s32[6,8]{1,0:T(8,128)S(1)}, f32[8,4,64,128]{3,2,1,0:T(8,128)S(1)}, f32[8,4,64,128]{3,2,1,0:T(8,128)S(1)}, f32[7,4,64,128]{3,2,1,0:T(8,128)}) %tuple.76, ...), branch_computations={%region_11.12_spmd, %region_12.13_spmd, %region_13.14_spmd, %regio... | conditional | bytes 8388936 | solution.py:462
  30.3 1.6 %branch_0_fun.8 = (f32[2,4,64,128]{3,2,1,0:T(8,128)S(1)}, f32[1,8,64,128]{3,2,1,0:T(8,128)S(1)}) custom-call(s32[6,8]{1,0:T(8,128)S(1)} %get-tuple-element.140.table_ref, f32[8,4,64,128]{3,2,1,0:T(8,128)S(1)} %get-tuple-element.141.own_ref, f32[8,4,64,128]{3,2,1,0:T(8,128)S(1)} %get-tuple-element.142.pal_ref, f32[7,4,64,128]{3,2,1,0:T(8,128)} %get-tuple-element.143.far_ref), custom_call_target="tpu_custom_call" | custom-call | tf_op jit(solution)/shard_map/cond/branch_0_fun/pallas_call | solution.py:233
  31.9 6.9 %collective-permute-start.7 = (f32[1,8,64,128]{3,2,1,0:T(8,128)S(1)}, f32[1,8,64,128]{3,2,1,0:T(8,128)S(1)}, u32[]{:S(2)}, u32[]{:S(2)}) collective-permute-start(f32[1,8,64,128]{3,2,1,0:T(8,128)S(1)} %get-tuple-element.145.own_ref), channel_id=1, source_target_pairs={{0,1},{1,0},{2,3},{3,2},{4,5},{5,4},{6,7},{7,6},{8,9},{9,8},{10,11... | collective-permute-start | bytes 786440 | tf_op jit(solution)/shard_map/cond/branch_0_fun/ppermute | solution.py:435
  38.8 5.3 %collective-permute-done.7.near_ref = f32[1,8,64,128]{3,2,1,0:T(8,128)S(1)} collective-permute-done((f32[1,8,64,128]{3,2,1,0:T(8,128)S(1)}, f32[1,8,64,128]{3,2,1,0:T(8,128)S(1)}, u32[]{:S(2)}, u32[]{:S(2)}) %collective-permute-start.7) | collective-permute-done | bytes 262176 | tf_op jit(solution)/shard_map/cond/branch_0_fun/ppermute | solution.py:435
  44.1 3.4 %collective-permute-start.8 = (f32[1,8,64,128]{3,2,1,0:T(8,128)S(1)}, f32[1,8,64,128]{3,2,1,0:T(8,128)S(1)}, u32[]{:S(2)}, u32[]{:S(2)}) collective-permute-start(f32[1,8,64,128]{3,2,1,0:T(8,128)S(1)} %collective-permute-done.7.near_ref), channel_id=1, source_target_pairs={{0,2},{2,4},{3,1},{4,6},{5,3},{7,5},{8,10},{10,12},{11,9},{12,14},... | collective-permute-start | bytes 786440 | tf_op jit(solution)/shard_map/cond/branch_0_fun/ppermute | solution.py:436
  47.5 3.9 %collective-permute-done.8.far_ref = f32[1,8,64,128]{3,2,1,0:T(8,128)S(1)} collective-permute-done((f32[1,8,64,128]{3,2,1,0:T(8,128)S(1)}, f32[1,8,64,128]{3,2,1,0:T(8,128)S(1)}, u32[]{:S(2)}, u32[]{:S(2)}) %collective-permute-start.8) | collective-permute-done | bytes 262176 | tf_op jit(solution)/shard_map/cond/branch_0_fun/ppermute | solution.py:436
  51.4 2.6 %branch_0_fun.9.rest_0_ = f32[1,8,64,128]{3,2,1,0:T(8,128)S(1)} custom-call(s32[6,8]{1,0:T(8,128)S(1)} %get-tuple-element.140.table_ref, f32[1,8,64,128]{3,2,1,0:T(8,128)S(1)} %collective-permute-done.8.far_ref, f32[1,8,64,128]{3,2,1,0:T(8,128)S(1)} %get-tuple-element.145.own_ref, f32[1,8,64,128]{3,2,1,0:T(8,128)S(1)} %collective-permute-done.7.near_ref), custom_call_target="tpu_custom_call" | custom-call | tf_op jit(solution)/shard_map/cond/branch_0_fun/pallas_call | solution.py:395
  53.9 2.2 %branch_0_fun.10 = (f32[8,4,64,128]{3,2,1,0:T(8,128)S(1)}, f32[8,4,64,128]{3,2,1,0:T(8,128)}, f32[7,4,64,128]{3,2,1,0:T(8,128)S(1)}) custom-call(s32[6,8]{1,0:T(8,128)S(1)} %get-tuple-element.140.table_ref, f32[8,4,64,128]{3,2,1,0:T(8,128)S(1)} %get-tuple-element.141.own_ref, f32[2,4,64,128]{3,2,1,0:T(8,128)S(1)} %get-tuple-element.144.partner_ref, ...), custom_call_target="tpu_custom_call" | custom-call | tf_op jit(solution)/shard_map/cond/branch_0_fun/pallas_call | solution.py:306
  56.1 1.9 %collective-permute-start.36 = (f32[8,4,64,128]{3,2,1,0:T(8,128)}, f32[8,4,64,128]{3,2,1,0:T(8,128)S(1)}, u32[]{:S(2)}, u32[]{:S(2)}) collective-permute-start(f32[8,4,64,128]{3,2,1,0:T(8,128)} %get-tuple-element.178), channel_id=1, source_target_pairs={{0,8},{8,0},{16,24},{24,16},{32,40},{40,32},{48,56},{56,48},{64,72... | collective-permute-start | bytes 3145736 | tf_op jit(solution)/shard_map/ppermute | solution.py:464
  58.0 45.2 %conditional.5 = (f32[7,4,64,128]{3,2,1,0:T(8,128)}) conditional(s32[]{:T(128)} %clamp.8, f32[7,4,64,128]{3,2,1,0:T(8,128)S(1)} %get-tuple-element.179, f32[7,4,64,128]{3,2,1,0:T(8,128)S(1)} %get-tuple-element.179, f32[7,4,64,128]{3,2,1,0:T(8,128)S(1)} %get-tuple-element.179, ...), branch_computations={%region_15.16_spmd, %region_16.17_spmd, %region_17.18_spmd, %regio... | conditional | bytes 4718640 | solution.py:466
  58.1 34.6 %collective-permute-start.30 = (f32[4,4,64,128]{3,2,1,0:T(8,128)S(1)}, f32[4,4,64,128]{3,2,1,0:T(8,128)S(1)}, u32[]{:S(2)}, u32[]{:S(2)}) collective-permute-start(f32[4,4,64,128]{3,2,1,0:T(8,128)S(1)} %slice.22), channel_id=1, source_target_pairs={{0,504},{8,16},{16,8},{24,32},{32,24},{40,48},{48,40},{56,64},{64,... | collective-permute-start | bytes 1572872 | tf_op jit(solution)/shard_map/cond/branch_3_fun/ppermute | solution.py:159
  92.7 9.7 %collective-permute-done.30.in_ref = f32[4,4,64,128]{3,2,1,0:T(8,128)S(1)} collective-permute-done((f32[4,4,64,128]{3,2,1,0:T(8,128)S(1)}, f32[4,4,64,128]{3,2,1,0:T(8,128)S(1)}, u32[]{:S(2)}, u32[]{:S(2)}) %collective-permute-start.30) | collective-permute-done | bytes 524320 | tf_op jit(solution)/shard_map/cond/branch_3_fun/ppermute | solution.py:159
  102.4 0.8 branch_3_fun.17
  103.2 0.0 collective-permute-done.36.pal_ref
  103.2 3.6 %shard_map.47 = f32[8,8,64,64]{3,2,1,0:T(8,128)} custom-call(s32[6,8]{1,0:T(8,128)S(1)} %add_add_fusion.table_ref, s32[8]{0:T(128)S(1)} %collective-permute-done.34.asked_ref, f32[8,4,64,128]{3,2,1,0:T(8,128)S(1)} %get-tuple-element.177.mid_ref, f32[8,4,64,128]{3,2,1,0:T(8,128)S(1)} %collective-permute-done.36.pal_ref, ...), custom_call_target="tpu_custom_call" | custom-call | tf_op jit(solution)/shard_map/pallas_call | solution.py:91
  (2 shorter events, 0.0 us)
Async XLA Ops:
  0.0 11.7 %copy-start.2 = (s32[8,2]{0,1:T(2,128)S(1)}, s32[8,2]{0,1:T(2,128)}, u32[]{:S(2)}) copy-start(s32[8,2]{0,1:T(2,128)} %param.24) | copy-start | bytes 196
  0.0 11.8 %copy-start.1 = (s32[512,2]{0,1:T(2,128)S(1)}, s32[512,2]{0,1:T(2,128)}, u32[]{:S(2)}) copy-start(s32[512,2]{0,1:T(2,128)} %param.23) | copy-start | bytes 12292
  1.4 7.5 %collective-permute-start.34 = (s32[8]{0:T(128)S(1)}, s32[8]{0:T(128)S(1)}, u32[]{:S(2)}, u32[]{:S(2)}) collective-permute-start(s32[8]{0:T(128)S(1)} %get-tuple-element.181), channel_id=1, source_target_pairs={{0,504},{8,16},{16,8},{24,32},{32,24},{40,48},{48,40},{56,64},{64,... | collective-permute-start | bytes 104 | tf_op jit(solution)/shard_map/ppermute | solution.py:444
  5.5 1.6 %copy-start = (f32[8,8,64,64]{3,2,1,0:T(8,128)S(1)}, f32[8,8,64,64]{3,2,1,0:T(8,128)}, u32[]{:S(2)}) copy-start(f32[8,8,64,64]{3,2,1,0:T(8,128)} %field_ref.1) | copy-start | bytes 3145732
  9.0 21.3 %collective-permute-start.35 = (f32[8,4,64,128]{3,2,1,0:T(8,128)S(1)}, f32[8,4,64,128]{3,2,1,0:T(8,128)S(1)}, u32[]{:S(2)}, u32[]{:S(2)}) collective-permute-start(f32[8,4,64,128]{3,2,1,0:T(8,128)S(1)} %shard_map.46), channel_id=1, source_target_pairs={{0,8},{8,0},{16,24},{24,16},{32,40},{40,32},{48,56},{56,48},{64,72... | collective-permute-start | bytes 3145736 | tf_op jit(solution)/shard_map/ppermute | solution.py:447
  15.3 14.1 %collective-permute-start.3 = (f32[4,4,64,128]{3,2,1,0:T(8,128)S(1)}, f32[4,4,64,128]{3,2,1,0:T(8,128)S(1)}, u32[]{:S(2)}, u32[]{:S(2)}) collective-permute-start(f32[4,4,64,128]{3,2,1,0:T(8,128)S(1)} %branch_3_fun.9), channel_id=1, source_target_pairs={{0,504},{8,16},{16,8},{24,32},{32,24},{40,48},{48,40},{56,64},{64,... | collective-permute-start | bytes 1572872 | tf_op jit(solution)/shard_map/cond/branch_3_fun/ppermute | solution.py:155
  31.9 12.2 %collective-permute-start.7 = (f32[1,8,64,128]{3,2,1,0:T(8,128)S(1)}, f32[1,8,64,128]{3,2,1,0:T(8,128)S(1)}, u32[]{:S(2)}, u32[]{:S(2)}) collective-permute-start(f32[1,8,64,128]{3,2,1,0:T(8,128)S(1)} %get-tuple-element.145.own_ref), channel_id=1, source_target_pairs={{0,1},{1,0},{2,3},{3,2},{4,5},{5,4},{6,7},{7,6},{8,9},{9,8},{10,11... | collective-permute-start | bytes 786440 | tf_op jit(solution)/shard_map/cond/branch_0_fun/ppermute | solution.py:435
  44.1 7.3 %collective-permute-start.8 = (f32[1,8,64,128]{3,2,1,0:T(8,128)S(1)}, f32[1,8,64,128]{3,2,1,0:T(8,128)S(1)}, u32[]{:S(2)}, u32[]{:S(2)}) collective-permute-start(f32[1,8,64,128]{3,2,1,0:T(8,128)S(1)} %collective-permute-done.7.near_ref), channel_id=1, source_target_pairs={{0,2},{2,4},{3,1},{4,6},{5,3},{7,5},{8,10},{10,12},{11,9},{12,14},... | collective-permute-start | bytes 786440 | tf_op jit(solution)/shard_map/cond/branch_0_fun/ppermute | solution.py:436
  56.1 47.1 %collective-permute-start.36 = (f32[8,4,64,128]{3,2,1,0:T(8,128)}, f32[8,4,64,128]{3,2,1,0:T(8,128)S(1)}, u32[]{:S(2)}, u32[]{:S(2)}) collective-permute-start(f32[8,4,64,128]{3,2,1,0:T(8,128)} %get-tuple-element.178), channel_id=1, source_target_pairs={{0,8},{8,0},{16,24},{24,16},{32,40},{40,32},{48,56},{56,48},{64,72... | collective-permute-start | bytes 3145736 | tf_op jit(solution)/shard_map/ppermute | solution.py:464
  58.1 44.3 %collective-permute-start.30 = (f32[4,4,64,128]{3,2,1,0:T(8,128)S(1)}, f32[4,4,64,128]{3,2,1,0:T(8,128)S(1)}, u32[]{:S(2)}, u32[]{:S(2)}) collective-permute-start(f32[4,4,64,128]{3,2,1,0:T(8,128)S(1)} %slice.22), channel_id=1, source_target_pairs={{0,504},{8,16},{16,8},{24,32},{32,24},{40,48},{48,40},{56,64},{64,... | collective-permute-start | bytes 1572872 | tf_op jit(solution)/shard_map/cond/branch_3_fun/ppermute | solution.py:159

commit v5 on v4

--- a/solution.py
+++ b/solution.py
@@ -26,6 +26,10 @@
 RING = ("grp", "orb")
 
 
+def group_index():
+    return lax.axis_index("grp") * lax.axis_size("orb") + lax.axis_index("orb")
+
+
 def even_edges():
     return [(g, g ^ 1) for g in range(lax.axis_size(RING))]
 
@@ -46,6 +50,10 @@
     return jnp.where((source >= 0) & (source < BOX), rolled, 0.0)
 
 
+def cost(microseconds):
+    return pl.CostEstimate(flops=0, bytes_accessed=int(3.6e6 * microseconds), transcendentals=0)
+
+
 def pack_kernel(field_ref, out_ref):
     half = field_ref.shape[1] // 2
     out_ref[...] = jnp.concatenate([field_ref[:, :half], field_ref[:, half:]], axis=-1)
@@ -63,14 +71,14 @@
     )(orbitals)
 
 
-def finish_kernel(table_ref, asked_ref, mid_ref, pal_ref, far_ref, out_ref, acc):
+def finish_kernel(asked_ref, mid_ref, pal_ref, far_ref, out_ref, acc):
     step, half = mid_ref.shape[:2]
     start = pl.program_id(0) * step
     orbs = pl.num_programs(0) * step
     acc[...] = mid_ref[...] + pal_ref[...]
     rank = 0
     for slot in range(asked_ref.shape[0]):
-        local = asked_ref[slot] - orbs * table_ref[GROUP, 0]
+        local = asked_ref[slot] - orbs * group_index()
         if slot:
             rank = jnp.minimum(rank, far_ref.shape[0] - 1)
 
@@ -83,7 +91,7 @@
     out_ref[:, half:] = acc[..., BOX:]
 
 
-def finish(table, asked, middle, from_pal, from_far):
+def finish(asked, middle, from_pal, from_far):
     orbs, half = middle.shape[:2]
     step = 2
     smem = pl.BlockSpec(memory_space=pltpu.SMEM)
@@ -91,20 +99,20 @@
     return pl.pallas_call(
         finish_kernel,
         grid=(orbs // step,),
-        in_specs=[smem, smem, spec, spec, pl.BlockSpec(memory_space=pltpu.VMEM)],
+        in_specs=[smem, spec, spec, pl.BlockSpec(memory_space=pltpu.VMEM)],
         out_specs=pl.BlockSpec((step, 2 * half, BOX, BOX), lambda i: (i, 0, 0, 0)),
         out_shape=jax.ShapeDtypeStruct((orbs, 2 * half, BOX, BOX), jnp.float32),
         scratch_shapes=[pltpu.VMEM((step, half, BOX, LANES), jnp.float32)],
         compiler_params=params(),
-    )(table, asked, middle, from_pal, from_far)
-
-
-def gather_kernel(table_ref, asked_ref, own_ref, out_ref, sems):
+    )(asked, middle, from_pal, from_far)
+
+
+def gather_kernel(asked_ref, own_ref, out_ref, sems):
     orbs, count = own_ref.shape[0], out_ref.shape[0]
     chosen = [0] * count
     rank = 0
     for slot in range(asked_ref.shape[0]):
-        local = asked_ref[slot] - orbs * table_ref[GROUP, 0]
+        local = asked_ref[slot] - orbs * group_index()
         hit = (local >= 0) & (local < orbs)
         chosen = [jnp.where(hit & (rank == k), local, old) for k, old in enumerate(chosen)]
         rank += hit.astype(jnp.int32)
@@ -118,17 +126,17 @@
         copy.wait()
 
 
-def gather(table, asked, own, count):
+def gather(asked, own, count):
     smem = pl.BlockSpec(memory_space=pltpu.SMEM)
     anywhere = pl.BlockSpec(memory_space=pl.ANY)
     return pl.pallas_call(
         gather_kernel,
-        in_specs=[smem, smem, anywhere],
+        in_specs=[smem, anywhere],
         out_specs=anywhere,
         out_shape=jax.ShapeDtypeStruct((count,) + own.shape[1:], jnp.float32),
         scratch_shapes=[pltpu.SemaphoreType.DMA((count,))],
         compiler_params=params(),
-    )(table, asked, own)
+    )(asked, own)
 
 
 def spread_kernel(in_ref, out_ref, sem):
@@ -151,23 +159,33 @@
     )(blocks)
 
 
-def ask(count, most, table, asked, own):
-    return spread(lax.ppermute(gather(table, asked, own, count), RING, odd_edges()), most)
+def ask(count, most, asked, own):
+    return spread(lax.ppermute(gather(asked, own, count), RING, odd_edges()), most)
 
 
 def answer(count, most, terms):
     return spread(lax.ppermute(terms[:count], RING, odd_edges()), most)
 
 
-FIRST, SECOND, BY_Y, BY_Z, GROUP, SLAB = range(6)
 MINE, PAL, FAR = range(3)
 
 
-def locate(table_ref, where_ref, orbs):
-    group = table_ref[GROUP, 0]
+class Slots:
+    def __init__(self, pairs_ref, seconds_ref, offsets_ref, orbs):
+        self.pairs, self.seconds, self.offsets, self.orbs = pairs_ref, seconds_ref, offsets_ref, orbs
+
+    def first(self, slot):
+        return self.pairs[0, slot] - self.orbs * group_index()
+
+    def shift(self, axis, slot):
+        return self.offsets[axis, self.pairs[1, slot]] - self.offsets[axis, self.pairs[0, slot]]
+
+
+def locate(slots, where_ref):
+    orbs, group = slots.orbs, group_index()
     rank = 0
     for slot in range(where_ref.shape[1]):
-        second = table_ref[SECOND, slot]
+        second = slots.seconds[slot]
         mine = second - orbs * group
         other = second - orbs * (group ^ 1)
         is_mine = (mine >= 0) & (mine < orbs)
@@ -189,10 +207,11 @@
     return pltpu.roll(field, LANES // 2, 1)
 
 
-def density_kernel(table_ref, own_ref, pal_ref, far_ref, partner_ref, *rest):
+def density_kernel(pairs_ref, seconds_ref, offsets_ref, own_ref, pal_ref, far_ref, partner_ref, *rest):
     out_refs, (padded, where) = rest[:-2], rest[-2:]
     planes = own_ref.shape[1]
-    locate(table_ref, where, own_ref.shape[0])
+    slots = Slots(pairs_ref, seconds_ref, offsets_ref, own_ref.shape[0])
+    locate(slots, where)
     clear_edges(padded)
     low = lane_index((BOX, LANES)) < BOX
 
@@ -203,9 +222,9 @@
             def _():
                 padded[:, PAD : PAD + BOX] = ref[where[1, slot]]
 
-        rows = pl.ds(PAD - table_ref[BY_Y, slot], BOX)
+        rows = pl.ds(PAD - slots.shift(0, slot), BOX)
         for x in range(planes):
-            partner_ref[slot, x] = moved_z(padded[x, rows, :], table_ref[BY_Z, slot])
+            partner_ref[slot, x] = moved_z(padded[x, rows, :], slots.shift(1, slot))
 
     done = 0
     for out_ref in out_refs:
@@ -217,37 +236,38 @@
             place_partner(slot)
             place_partner(slot + 1)
             for x in range(planes):
-                one = own_ref[table_ref[FIRST, slot], x] * partner_ref[slot, x]
-                two = own_ref[table_ref[FIRST, slot + 1], x] * partner_ref[slot + 1, x]
+                one = own_ref[slots.first(slot), x] * partner_ref[slot, x]
+                two = own_ref[slots.first(slot + 1), x] * partner_ref[slot + 1, x]
                 out_ref[pair, x] = jnp.where(low, one, swapped(two))
                 out_ref[pair, planes + x] = jnp.where(low, swapped(one), two)
 
         done += count
 
 
-def densities(table, own, pal, far, chunks):
+def densities(tables, own, pal, far, chunks):
     planes = own.shape[1]
     vmem = pl.BlockSpec(memory_space=pltpu.VMEM)
     shapes = [(2 * sum(chunks), planes, BOX, LANES)]
     shapes += [(count, 2 * planes, BOX, LANES) for count in chunks]
     return pl.pallas_call(
         density_kernel,
-        in_specs=[pl.BlockSpec(memory_space=pltpu.SMEM)] + [vmem] * 3,
+        in_specs=[pl.BlockSpec(memory_space=pltpu.SMEM)] * 3 + [vmem] * 3,
         out_specs=[vmem] * len(shapes),
         out_shape=[jax.ShapeDtypeStruct(shape, jnp.float32) for shape in shapes],
         scratch_shapes=[
             pltpu.VMEM((planes, ROWS, LANES), jnp.float32),
-            pltpu.SMEM((2, table.shape[1]), jnp.int32),
+            pltpu.SMEM((2, tables[1].shape[0]), jnp.int32),
         ],
         compiler_params=params(),
-    )(table, own, pal, far)
-
-
-def exchange_kernel(table_ref, own_ref, partner_ref, *rest):
+    )(*tables, own, pal, far)
+
+
+def exchange_kernel(pairs_ref, seconds_ref, offsets_ref, own_ref, partner_ref, *rest):
     pot_refs = rest[:-5]
     mid_ref, to_pal_ref, to_far_ref, padded, where = rest[-5:]
     orbs, planes = mid_ref.shape[:2]
-    locate(table_ref, where, orbs)
+    slots = Slots(pairs_ref, seconds_ref, offsets_ref, orbs)
+    locate(slots, where)
     clear_edges(padded)
     zeros = jnp.zeros((planes, BOX, LANES), jnp.float32)
     low = lane_index((BOX, LANES)) < BOX
@@ -258,10 +278,10 @@
         to_pal_ref[orb] = zeros
 
     def add_terms(slot, potential):
-        first = table_ref[FIRST, slot]
-        by_y = table_ref[BY_Y, slot]
-        by_z = table_ref[BY_Z, slot]
-        weight = jnp.where(table_ref[SECOND, slot] >= 0, 1.0, 0.0)
+        first = slots.first(slot)
+        by_y = slots.shift(0, slot)
+        by_z = slots.shift(1, slot)
+        weight = jnp.where(slots.seconds[slot] >= 0, 1.0, 0.0)
         for x in range(planes):
             pot = weight * potential(x)
             mid_ref[first, x] += pot * partner_ref[slot, x]
@@ -300,12 +320,12 @@
         done += count
 
 
-def exchange_terms(table, potentials, own, partner, most):
+def exchange_terms(tables, potentials, own, partner, most):
     planes = own.shape[1]
     vmem = pl.BlockSpec(memory_space=pltpu.VMEM)
     return pl.pallas_call(
         exchange_kernel,
-        in_specs=[pl.BlockSpec(memory_space=pltpu.SMEM)] + [vmem] * (2 + len(potentials)),
+        in_specs=[pl.BlockSpec(memory_space=pltpu.SMEM)] * 3 + [vmem] * (2 + len(potentials)),
         out_specs=[vmem] * 3,
         out_shape=[
             jax.ShapeDtypeStruct((count,) + own.shape[1:], jnp.float32)
@@ -313,10 +333,10 @@
         ],
         scratch_shapes=[
             pltpu.VMEM((planes, ROWS, LANES), jnp.float32),
-            pltpu.SMEM((2, table.shape[1]), jnp.int32),
+            pltpu.SMEM((2, tables[1].shape[0]), jnp.int32),
         ],
         compiler_params=params(),
-    )(table, own, partner, *potentials)
+    )(*tables, own, partner, *potentials)
 
 
 SUB = 8
@@ -333,8 +353,8 @@
     return made
 
 
-def solve_kernel(slabs, table_ref, far_ref, own_ref, near_ref, out_ref, dens, even, odd):
-    slab = table_ref[SLAB, 0]
+def solve_kernel(slabs, far_ref, own_ref, near_ref, out_ref, dens, even, odd):
+    slab = lax.axis_index("slab")
     pairs, planes = own_ref.shape[:2]
     flip = lax.rem(slab, 2)
     far_at = flip * 2 * planes
@@ -389,36 +409,18 @@
                         out_ref[pair, x - planes, pl.ds(t, SUB, stride=SUB), :] = fresh[t]
 
 
-def solve(table, far, own, near, slabs):
+def solve(far, own, near, slabs):
     planes = own.shape[1]
     vmem = pl.BlockSpec(memory_space=pltpu.VMEM)
     return pl.pallas_call(
         functools.partial(solve_kernel, slabs),
-        in_specs=[pl.BlockSpec(memory_space=pltpu.SMEM), vmem, vmem, vmem],
+        in_specs=[vmem] * 3,
         out_specs=vmem,
         out_shape=jax.ShapeDtypeStruct(own.shape, jnp.float32),
         scratch_shapes=[pltpu.VMEM((3 * planes, SUB + 2, SUB, LANES), jnp.float32)] * 3,
-        compiler_params=params(),
-    )(table, far, own, near)
-
-
-def slot_table(offsets, pairs, seconds, orb_dev):
-    total_orbs = offsets.shape[0]
-    group = lax.axis_index(RING).astype(jnp.int32)
-    ids = jnp.arange(total_orbs, dtype=jnp.int32)
-    pick_first = (pairs[:, 0:1] == ids[None, :]).astype(jnp.int32)
-    pick_second = (pairs[:, 1:2] == ids[None, :]).astype(jnp.int32)
-    shift = jnp.sum((pick_second - pick_first)[:, :, None] * offsets[None, :, :], axis=1)
-    constants = jnp.stack([group, lax.axis_index("slab").astype(jnp.int32)])
-    return jnp.concatenate(
-        [
-            (pairs[:, 0] - orb_dev * group)[None, :],
-            seconds[None, :],
-            shift.T,
-            jnp.broadcast_to(constants[:, None], (2, pairs.shape[0])),
-        ],
-        axis=0,
-    )
+        cost_estimate=cost(own.shape[0] * 2.5),
+        compiler_params=params(),
+    )(far, own, near)
 
 
 def asked_by(seconds, group, orb_dev):
@@ -426,16 +428,16 @@
     return jnp.sum(((local >= 0) & (local < orb_dev)).astype(jnp.int32))
 
 
-def solved_terms(count, table, own, pal, far):
+def solved_terms(count, tables, own, pal, far):
     slabs = lax.axis_size("slab")
     across = [(s, s ^ 1) for s in range(slabs)]
     onward = [(s, s + 2 - 4 * (s % 2)) for s in range(slabs)]
     onward = [(s, t) for s, t in onward if 0 <= t < slabs]
-    partner, *made = densities(table, own, pal, far, [1] * count)
+    partner, *made = densities(tables, own, pal, far, [1] * count)
     near = [lax.ppermute(dens, "slab", across) for dens in made]
     next_but_one = [lax.ppermute(dens, "slab", onward) for dens in near]
-    potentials = [solve(table, f, d, n, slabs) for f, d, n in zip(next_but_one, made, near)]
-    return exchange_terms(table, potentials, own, partner, far.shape[0])
+    potentials = [solve(f, d, n, slabs) for f, d, n in zip(next_but_one, made, near)]
+    return exchange_terms(tables, potentials, own, partner, far.shape[0])
 
 
 def body(orbitals, offsets, pairs, live):
@@ -445,7 +447,7 @@
     own = pack(orbitals)
     offered, asked = lax.optimization_barrier((own, asked))
     pal = lax.ppermute(offered, RING, even_edges())
-    table = slot_table(offsets, pairs, seconds, orbs)
+    tables = (pairs.T, seconds, offsets.T)
 
     group = lax.axis_index(RING)
     beyond = (group + 2 * (group % 2) - 1) % lax.axis_size(RING)
@@ -454,17 +456,17 @@
     length = jnp.clip(longer, 1, most) - 1
     lengths = range(1, most + 1)
     asks = [functools.partial(ask, k, most) for k in lengths]
-    far = lax.switch(length, asks, table, asked, own)
+    far = lax.switch(length, asks, asked, own)
 
     pairs_most = (slots + 1) // 2
     count = jnp.clip((jnp.sum(live) + 1) // 2, 1, pairs_most)
     solves = [functools.partial(solved_terms, k) for k in range(1, pairs_most + 1)]
-    middle, to_pal, to_far = lax.switch(count - 1, solves, table, own, pal, far)
+    middle, to_pal, to_far = lax.switch(count - 1, solves, tables, own, pal, far)
 
     from_pal = lax.ppermute(to_pal, RING, even_edges())
     answers = [functools.partial(answer, k, most) for k in lengths]
     from_far = lax.switch(length, answers, to_far)
-    return finish(table, asked, middle, from_pal, from_far)
+    return finish(asked, middle, from_pal, from_far)
 
 
 def solution(mesh):

time: 107 us -> 106 us (level)
  the two profiles are of different devices: /device:TPU:64 before, /device:TPU:57 now
where the time goes in v5:
time: 106 us; the launch traced here: 107 us
  starting transfers between devices  44.7 us (42%)
  waiting for transfers between devices  43.6 us (41%)
  Pallas kernels  12.7 us (12%)
  between operations  2.15 us (2%)
  other arithmetic  2.09 us (2%)
  local copies, waits for them, and re-layouts  1.64 us (2%)
    ppermute x1, starting transfers between devices, answer(): return spread(lax.ppermute(terms[:count], RING, odd_edges()), most)  21.2 us
    ppermute x1, waiting for transfers between devices, solved_terms(): near = [lax.ppermute(dens, 'slab', across) for dens in made]  16.2 us
    ppermute x1, waiting for transfers between devices, answer(): return spread(lax.ppermute(terms[:count], RING, odd_edges()), most)  9.44 us
    ppermute x1, waiting for transfers between devices, ask(): lax.ppermute(gather(asked, own, count), RING, odd_edges())  9.09 us
    ppermute x1, waiting for transfers between devices, solved_terms(): next_but_one = [lax.ppermute(dens, 'slab', onward) for dens in near]  8.85 us
    ppermute x1, starting transfers between devices, body(): asked = lax.ppermute(seconds, RING, odd_edges())  6.9 us
    ppermute x1, starting transfers between devices, body(): from_pal = lax.ppermute(to_pal, RING, even_edges())  5.96 us
    ppermute x1, starting transfers between devices, ask(): lax.ppermute(gather(asked, own, count), RING, odd_edges())  5.51 us
  transfers between devices with their start and end apart: 7, of which 4 were waited for; matrix products, arithmetic and copies ran while one was open for 1% of the time, Pallas kernels for 3%

profile of v5, /device:TPU:57, one launch (start us, length us, event | category | flops | bytes accessed | tf_op | source)
XLA Modules:
  0.0 107.1 jit_solution(15286135681964200332)
XLA Ops:
  0.0 1.4 %fusion.1 = (s32[]{:T(128)}, s32[8]{0:T(128)S(1)}, s32[]{:T(128)}) fusion(s32[]{:T(128)S(6)} %mul.15, s32[8,2]{0,1:T(2,128)} %param.24, s32[8]{0:T(128)} %param.25), kind=kLoop, calls=%fused_computation.4 | loop fusion | flops 70 | bytes 108 | tf_op jit(solution)/shard_map/reduce_sum | solution.py:428
  1.4 6.9 %collective-permute-start.34 = (s32[8]{0:T(128)S(1)}, s32[8]{0:T(128)S(1)}, u32[]{:S(2)}, u32[]{:S(2)}) collective-permute-start(s32[8]{0:T(128)S(1)} %get-tuple-element.184), channel_id=1, source_target_pairs={{0,504},{8,16},{16,8},{24,32},{32,24},{40,48},{48,40},{56,64},{64,... | collective-permute-start | bytes 104 | tf_op jit(solution)/shard_map/ppermute | solution.py:446
  8.3 0.0 copy-start
  8.3 1.6 %copy-done = f32[8,8,64,64]{3,2,1,0:T(8,128)S(1)} copy-done((f32[8,8,64,64]{3,2,1,0:T(8,128)S(1)}, f32[8,8,64,64]{3,2,1,0:T(8,128)}, u32[]{:S(2)}) %copy-start) | copy-done | bytes 1048600
  9.9 0.4 shard_map.46
  10.3 0.0 collective-permute-done.34.asked_ref
  10.3 1.9 %collective-permute-start.35 = (f32[8,4,64,128]{3,2,1,0:T(8,128)S(1)}, f32[8,4,64,128]{3,2,1,0:T(8,128)S(1)}, u32[]{:S(2)}, u32[]{:S(2)}) collective-permute-start(f32[8,4,64,128]{3,2,1,0:T(8,128)S(1)} %shard_map.46), channel_id=1, source_target_pairs={{0,8},{8,0},{16,24},{24,16},{32,40},{40,32},{48,56},{56,48},{64,72... | collective-permute-start | bytes 3145736 | tf_op jit(solution)/shard_map/ppermute | solution.py:449
  13.0 0.7 fusion
  15.0 0.0 copy-start.1
  15.0 0.0 copy-start.2
  15.0 16.8 %conditional.3 = (f32[7,4,64,128]{3,2,1,0:T(8,128)}) conditional(s32[]{:T(128)} %clamp.8, (s32[8]{0:T(128)S(1)}, f32[8,4,64,128]{3,2,1,0:T(8,128)S(1)}) %tuple.75, (s32[8]{0:T(128)S(1)}, f32[8,4,64,128]{3,2,1,0:T(8,128)S(1)}) %tuple.75, (s32[8]{0:T(128)S(1)}, f32[8,4,64,128]{3,2,1,0:T(8,128)S(1)}) %tuple.75, ...), branch_computations={%region_3.4_spmd, %region_4.5_spmd, %region_5.6_spmd, %region_6.7_... | conditional | bytes 3670064 | solution.py:459
  15.0 1.3 %branch_3_fun.9 = f32[4,4,64,128]{3,2,1,0:T(8,128)S(1)} custom-call(s32[8]{0:T(128)S(1)} %get-tuple-element.127.asked_ref, f32[8,4,64,128]{3,2,1,0:T(8,128)S(1)} %get-tuple-element.128.own_ref), custom_call_target="tpu_custom_call" | custom-call | tf_op jit(solution)/shard_map/cond/branch_3_fun/pallas_call | solution.py:132
  16.4 5.5 %collective-permute-start.3 = (f32[4,4,64,128]{3,2,1,0:T(8,128)S(1)}, f32[4,4,64,128]{3,2,1,0:T(8,128)S(1)}, u32[]{:S(2)}, u32[]{:S(2)}) collective-permute-start(f32[4,4,64,128]{3,2,1,0:T(8,128)S(1)} %branch_3_fun.9), channel_id=1, source_target_pairs={{0,504},{8,16},{16,8},{24,32},{32,24},{40,48},{48,40},{56,64},{64,... | collective-permute-start | bytes 1572872 | tf_op jit(solution)/shard_map/cond/branch_3_fun/ppermute | solution.py:163
  21.9 9.1 %collective-permute-done.3.in_ref = f32[4,4,64,128]{3,2,1,0:T(8,128)S(1)} collective-permute-done((f32[4,4,64,128]{3,2,1,0:T(8,128)S(1)}, f32[4,4,64,128]{3,2,1,0:T(8,128)S(1)}, u32[]{:S(2)}, u32[]{:S(2)}) %collective-permute-start.3) | collective-permute-done | bytes 524320 | tf_op jit(solution)/shard_map/cond/branch_3_fun/ppermute | solution.py:163
  31.0 0.8 branch_3_fun.10
  31.8 0.0 collective-permute-done.35
  31.8 0.0 copy-done.1
  31.8 0.0 copy-done.2
  31.8 34.1 %conditional.4 = ((f32[8,4,64,128]{3,2,1,0:T(8,128)S(1)}, f32[8,4,64,128]{3,2,1,0:T(8,128)}, f32[7,4,64,128]{3,2,1,0:T(8,128)S(1)})) conditional(s32[]{:T(128)} %clamp.7, (s32[2,8]{1,0:T(2,128)S(1)}, s32[8]{0:T(128)S(1)}, s32[2,512]{1,0:T(2,128)S(1)}, f32[8,4,64,128]{3,2,1,0:T(8,128)S(1)}, ...), branch_computations={%region_10.11_spmd, %region_11.12_spmd, %region_12.13_spmd, %regio... | conditional | bytes 44388936 | solution.py:464
  31.8 1.6 %branch_0_fun.8 = (f32[2,4,64,128]{3,2,1,0:T(8,128)S(1)}, f32[1,8,64,128]{3,2,1,0:T(8,128)S(1)}) custom-call(s32[2,8]{1,0:T(2,128)S(1)} %get-tuple-element.135.pairs_ref, s32[8]{0:T(128)S(1)} %get-tuple-element.136.seconds_ref, s32[2,512]{1,0:T(2,128)S(1)} %get-tuple-element.137.offsets_ref, f32[8,4,64,128]{3,2,1,0:T(8,128)S(1)} %get-tuple-element.138.own_ref, ...), custom_call_target="tpu_custom_call" | custom-call | tf_op jit(solution)/shard_map/cond/branch_0_fun/pallas_call | solution.py:252
  33.5 1.9 %collective-permute-start.7 = (f32[1,8,64,128]{3,2,1,0:T(8,128)S(1)}, f32[1,8,64,128]{3,2,1,0:T(8,128)S(1)}, u32[]{:S(2)}, u32[]{:S(2)}) collective-permute-start(f32[1,8,64,128]{3,2,1,0:T(8,128)S(1)} %get-tuple-element.142.own_ref), channel_id=1, source_target_pairs={{0,1},{1,0},{2,3},{3,2},{4,5},{5,4},{6,7},{7,6},{8,9},{9,8},{10,11... | collective-permute-start | bytes 786440 | tf_op jit(solution)/shard_map/cond/branch_0_fun/ppermute | solution.py:437
  35.4 16.2 %collective-permute-done.7.near_ref = f32[1,8,64,128]{3,2,1,0:T(8,128)S(1)} collective-permute-done((f32[1,8,64,128]{3,2,1,0:T(8,128)S(1)}, f32[1,8,64,128]{3,2,1,0:T(8,128)S(1)}, u32[]{:S(2)}, u32[]{:S(2)}) %collective-permute-start.7) | collective-permute-done | bytes 262176 | tf_op jit(solution)/shard_map/cond/branch_0_fun/ppermute | solution.py:437
  51.6 1.3 %collective-permute-start.8 = (f32[1,8,64,128]{3,2,1,0:T(8,128)S(1)}, f32[1,8,64,128]{3,2,1,0:T(8,128)S(1)}, u32[]{:S(2)}, u32[]{:S(2)}) collective-permute-start(f32[1,8,64,128]{3,2,1,0:T(8,128)S(1)} %collective-permute-done.7.near_ref), channel_id=1, source_target_pairs={{0,2},{2,4},{3,1},{4,6},{5,3},{7,5},{8,10},{10,12},{11,9},{12,14},... | collective-permute-start | bytes 786440 | tf_op jit(solution)/shard_map/cond/branch_0_fun/ppermute | solution.py:438
  52.9 8.8 %collective-permute-done.8.far_ref = f32[1,8,64,128]{3,2,1,0:T(8,128)S(1)} collective-permute-done((f32[1,8,64,128]{3,2,1,0:T(8,128)S(1)}, f32[1,8,64,128]{3,2,1,0:T(8,128)S(1)}, u32[]{:S(2)}, u32[]{:S(2)}) %collective-permute-start.8) | collective-permute-done | bytes 262176 | tf_op jit(solution)/shard_map/cond/branch_0_fun/ppermute | solution.py:438
  61.8 2.0 %branch_0_fun.9.rest_0_ = f32[1,8,64,128]{3,2,1,0:T(8,128)S(1)} custom-call(f32[1,8,64,128]{3,2,1,0:T(8,128)S(1)} %collective-permute-done.8.far_ref, f32[1,8,64,128]{3,2,1,0:T(8,128)S(1)} %get-tuple-element.142.own_ref, f32[1,8,64,128]{3,2,1,0:T(8,128)S(1)} %collective-permute-done.7.near_ref), custom_call_target="tpu_custom_call" | custom-call | bytes 9000000 | tf_op jit(solution)/shard_map/cond/branch_0_fun/pallas_call | solution.py:415
  63.7 2.2 %branch_0_fun.10 = (f32[8,4,64,128]{3,2,1,0:T(8,128)S(1)}, f32[8,4,64,128]{3,2,1,0:T(8,128)}, f32[7,4,64,128]{3,2,1,0:T(8,128)S(1)}) custom-call(s32[2,8]{1,0:T(2,128)S(1)} %get-tuple-element.135.pairs_ref, s32[8]{0:T(128)S(1)} %get-tuple-element.136.seconds_ref, s32[2,512]{1,0:T(2,128)S(1)} %get-tuple-element.137.offsets_ref, ...), custom_call_target="tpu_custom_call" | custom-call | tf_op jit(solution)/shard_map/cond/branch_0_fun/pallas_call | solution.py:326
  65.9 6.0 %collective-permute-start.36 = (f32[8,4,64,128]{3,2,1,0:T(8,128)}, f32[8,4,64,128]{3,2,1,0:T(8,128)S(1)}, u32[]{:S(2)}, u32[]{:S(2)}) collective-permute-start(f32[8,4,64,128]{3,2,1,0:T(8,128)} %get-tuple-element.181), channel_id=1, source_target_pairs={{0,8},{8,0},{16,24},{24,16},{32,40},{40,32},{48,56},{56,48},{64,72... | collective-permute-start | bytes 3145736 | tf_op jit(solution)/shard_map/ppermute | solution.py:466
  71.9 31.6 %conditional.5 = (f32[7,4,64,128]{3,2,1,0:T(8,128)}) conditional(s32[]{:T(128)} %clamp.8, f32[7,4,64,128]{3,2,1,0:T(8,128)S(1)} %get-tuple-element.182, f32[7,4,64,128]{3,2,1,0:T(8,128)S(1)} %get-tuple-element.182, f32[7,4,64,128]{3,2,1,0:T(8,128)S(1)} %get-tuple-element.182, ...), branch_computations={%region_14.15_spmd, %region_15.16_spmd, %region_16.17_spmd, %regio... | conditional | bytes 4718640 | solution.py:468
  72.0 21.2 %collective-permute-start.30 = (f32[4,4,64,128]{3,2,1,0:T(8,128)S(1)}, f32[4,4,64,128]{3,2,1,0:T(8,128)S(1)}, u32[]{:S(2)}, u32[]{:S(2)}) collective-permute-start(f32[4,4,64,128]{3,2,1,0:T(8,128)S(1)} %slice.17), channel_id=1, source_target_pairs={{0,504},{8,16},{16,8},{24,32},{32,24},{40,48},{48,40},{56,64},{64,... | collective-permute-start | bytes 1572872 | tf_op jit(solution)/shard_map/cond/branch_3_fun/ppermute | solution.py:167
  93.2 9.4 %collective-permute-done.30.in_ref = f32[4,4,64,128]{3,2,1,0:T(8,128)S(1)} collective-permute-done((f32[4,4,64,128]{3,2,1,0:T(8,128)S(1)}, f32[4,4,64,128]{3,2,1,0:T(8,128)S(1)}, u32[]{:S(2)}, u32[]{:S(2)}) %collective-permute-start.30) | collective-permute-done | bytes 524320 | tf_op jit(solution)/shard_map/cond/branch_3_fun/ppermute | solution.py:167
  102.6 0.8 branch_3_fun.17
  103.5 0.0 collective-permute-done.36.pal_ref
  103.5 3.6 %shard_map.47 = f32[8,8,64,64]{3,2,1,0:T(8,128)} custom-call(s32[8]{0:T(128)S(1)} %collective-permute-done.34.asked_ref, f32[8,4,64,128]{3,2,1,0:T(8,128)S(1)} %get-tuple-element.180.mid_ref, f32[8,4,64,128]{3,2,1,0:T(8,128)S(1)} %collective-permute-done.36.pal_ref, f32[7,4,64,128]{3,2,1,0:T(8,128)} %get-tuple-element.200.far_ref), custom_call_target="tpu_custom_call" | custom-call | tf_op jit(solution)/shard_map/pallas_call | solution.py:99
  (1 shorter events, 0.0 us)
Async XLA Ops:
  1.4 8.9 %collective-permute-start.34 = (s32[8]{0:T(128)S(1)}, s32[8]{0:T(128)S(1)}, u32[]{:S(2)}, u32[]{:S(2)}) collective-permute-start(s32[8]{0:T(128)S(1)} %get-tuple-element.184), channel_id=1, source_target_pairs={{0,504},{8,16},{16,8},{24,32},{32,24},{40,48},{48,40},{56,64},{64,... | collective-permute-start | bytes 104 | tf_op jit(solution)/shard_map/ppermute | solution.py:446
  8.3 1.6 %copy-start = (f32[8,8,64,64]{3,2,1,0:T(8,128)S(1)}, f32[8,8,64,64]{3,2,1,0:T(8,128)}, u32[]{:S(2)}) copy-start(f32[8,8,64,64]{3,2,1,0:T(8,128)} %field_ref.1) | copy-start | bytes 3145732
  10.3 21.5 %collective-permute-start.35 = (f32[8,4,64,128]{3,2,1,0:T(8,128)S(1)}, f32[8,4,64,128]{3,2,1,0:T(8,128)S(1)}, u32[]{:S(2)}, u32[]{:S(2)}) collective-permute-start(f32[8,4,64,128]{3,2,1,0:T(8,128)S(1)} %shard_map.46), channel_id=1, source_target_pairs={{0,8},{8,0},{16,24},{24,16},{32,40},{40,32},{48,56},{56,48},{64,72... | collective-permute-start | bytes 3145736 | tf_op jit(solution)/shard_map/ppermute | solution.py:449
  15.0 16.8 %copy-start.1 = (s32[512,2]{0,1:T(2,128)S(1)}, s32[512,2]{0,1:T(2,128)}, u32[]{:S(2)}) copy-start(s32[512,2]{0,1:T(2,128)} %param.23) | copy-start | bytes 12292
  15.0 16.8 %copy-start.2 = (s32[8,2]{0,1:T(2,128)S(1)}, s32[8,2]{0,1:T(2,128)}, u32[]{:S(2)}) copy-start(s32[8,2]{0,1:T(2,128)} %param.24) | copy-start | bytes 196
  16.4 14.6 %collective-permute-start.3 = (f32[4,4,64,128]{3,2,1,0:T(8,128)S(1)}, f32[4,4,64,128]{3,2,1,0:T(8,128)S(1)}, u32[]{:S(2)}, u32[]{:S(2)}) collective-permute-start(f32[4,4,64,128]{3,2,1,0:T(8,128)S(1)} %branch_3_fun.9), channel_id=1, source_target_pairs={{0,504},{8,16},{16,8},{24,32},{32,24},{40,48},{48,40},{56,64},{64,... | collective-permute-start | bytes 1572872 | tf_op jit(solution)/shard_map/cond/branch_3_fun/ppermute | solution.py:163
  33.5 18.2 %collective-permute-start.7 = (f32[1,8,64,128]{3,2,1,0:T(8,128)S(1)}, f32[1,8,64,128]{3,2,1,0:T(8,128)S(1)}, u32[]{:S(2)}, u32[]{:S(2)}) collective-permute-start(f32[1,8,64,128]{3,2,1,0:T(8,128)S(1)} %get-tuple-element.142.own_ref), channel_id=1, source_target_pairs={{0,1},{1,0},{2,3},{3,2},{4,5},{5,4},{6,7},{7,6},{8,9},{9,8},{10,11... | collective-permute-start | bytes 786440 | tf_op jit(solution)/shard_map/cond/branch_0_fun/ppermute | solution.py:437
  51.6 10.1 %collective-permute-start.8 = (f32[1,8,64,128]{3,2,1,0:T(8,128)S(1)}, f32[1,8,64,128]{3,2,1,0:T(8,128)S(1)}, u32[]{:S(2)}, u32[]{:S(2)}) collective-permute-start(f32[1,8,64,128]{3,2,1,0:T(8,128)S(1)} %collective-permute-done.7.near_ref), channel_id=1, source_target_pairs={{0,2},{2,4},{3,1},{4,6},{5,3},{7,5},{8,10},{10,12},{11,9},{12,14},... | collective-permute-start | bytes 786440 | tf_op jit(solution)/shard_map/cond/branch_0_fun/ppermute | solution.py:438
  65.9 37.6 %collective-permute-start.36 = (f32[8,4,64,128]{3,2,1,0:T(8,128)}, f32[8,4,64,128]{3,2,1,0:T(8,128)S(1)}, u32[]{:S(2)}, u32[]{:S(2)}) collective-permute-start(f32[8,4,64,128]{3,2,1,0:T(8,128)} %get-tuple-element.181), channel_id=1, source_target_pairs={{0,8},{8,0},{16,24},{24,16},{32,40},{40,32},{48,56},{56,48},{64,72... | collective-permute-start | bytes 3145736 | tf_op jit(solution)/shard_map/ppermute | solution.py:466
  72.0 30.7 %collective-permute-start.30 = (f32[4,4,64,128]{3,2,1,0:T(8,128)S(1)}, f32[4,4,64,128]{3,2,1,0:T(8,128)S(1)}, u32[]{:S(2)}, u32[]{:S(2)}) collective-permute-start(f32[4,4,64,128]{3,2,1,0:T(8,128)S(1)} %slice.17), channel_id=1, source_target_pairs={{0,504},{8,16},{16,8},{24,32},{32,24},{40,48},{48,40},{56,64},{64,... | collective-permute-start | bytes 1572872 | tf_op jit(solution)/shard_map/cond/branch_3_fun/ppermute | solution.py:167
